TPU v7x, 32 devices: a whole 2x2x4 slice. The times are simulated.
32 devices in a mesh: mom: 2 (over y), shard: 16 (over z, x, core).
Axes of the slice: x: 2, y: 2, z: 4, core: 2. Of those that a mesh axis runs over, the one named last changes fastest.
Arguments:
- green_ret: bfloat16 [2, 256, 8, 2, 128, 128], P('mom', 'shard'), may hold values from -4 to 4
- broadening: bfloat16 [2, 128, 128], replicated, may hold values from -0.5 to 0.5
- occupation: float32 [2, 256], P('mom', 'shard'), may hold values from 0.1 to 1
- neighbours: int32 [64, 4], replicated, may hold values from 0 to 63, as said below
- orbitals: int32 [64], replicated, may hold values from 4 to 16
- coupling: bfloat16 [64, 4, 256, 256], P('shard'), may hold values from -0.1875 to 0.1875
- phonon: float32 [8, 2, 256], replicated, may hold values from -5 to 5
- mode_table: int32 [2, 2], replicated, may hold values from 0 to 7, as said below
Outputs:
- self_energy: bfloat16 [2, 256, 64, 2, 256], P('mom', None, 'shard')
Inputs may be any that keep to these rules, and one draw needn't show every extreme that they name: `neighbours`: row a holds 4 distinct atoms of a's own layer block (atoms 8 * (a // 8) onward), none equal to a; the first is a with its lowest bit flipped. `mode_table`: each entry names one of the 8 phonon modes.
All inputs are finite; a program needn't handle non-finite values.
Results may differ from a plain program's by a relative error of at most 0.013.
Values may be sent and summed in bfloat16 or wider, within the bound.
A program may use at most 192 MiB of HBM per device.

v0:
```python
import math

import jax
import jax.numpy as jnp
from jax import lax
from jax.sharding import PartitionSpec as P

NORB = 16
ATL = 8
NBR = 4
ENERGIES = 256
LAYERS = 8
ORB = 128
PAIR = 256
ATOMS = 64


def dft_tables(length):
    counter = jnp.arange(length, dtype=jnp.int32)
    phases = counter[:, None] * counter[None, :] % length
    angles = phases.astype(jnp.float32) * (2.0 * math.pi / length)
    return (jnp.cos(angles).astype(jnp.bfloat16), jnp.sin(angles).astype(jnp.bfloat16))


def local(green_ret, broadening, occupation, neighbours, orbitals, coupling, phonon, mode_table):
    highest = lax.Precision.HIGHEST
    greens = green_ret[0]
    energy_dev = greens.shape[0]
    mixing = jnp.stack(
        [
            jnp.concatenate([broadening[0], broadening[1]], axis=1),
            jnp.concatenate([-broadening[1], broadening[0]], axis=1),
        ],
        axis=0,
    )
    left = jnp.einsum("elpik,pkq->eliq", greens, mixing, preferred_element_type=jnp.float32).astype(
        jnp.bfloat16
    )
    slot_atoms = neighbours % ATL
    selector = slot_atoms[:, :, None] == jnp.arange(ATL, dtype=jnp.int32)[None, None, :]
    layer_orbitals = jnp.repeat(orbitals.reshape(LAYERS, ATL), ATL, axis=0)
    partner_count = jnp.sum(jnp.where(selector, layer_orbitals[:, None, :], 0), axis=2)
    green_rows = greens.reshape(energy_dev, LAYERS, 2, ATL, NORB, ORB)
    select_bf = selector.reshape(LAYERS, ATL, NBR, ATL).astype(jnp.bfloat16)
    partner_rows = jnp.einsum(
        "ljnm,elpmic->eljnpic", select_bf, green_rows, preferred_element_type=jnp.float32
    ).astype(jnp.bfloat16)
    partner_re = partner_rows[:, :, :, :, 0]
    partner_im = partner_rows[:, :, :, :, 1]
    left_rows_re = left[..., :ORB].reshape(energy_dev, LAYERS, ATL, NORB, ORB)
    left_rows_im = left[..., ORB:].reshape(energy_dev, LAYERS, ATL, NORB, ORB)
    pair_re = jnp.einsum(
        "eljic,eljnkc->eljnik", left_rows_re, partner_re, preferred_element_type=jnp.float32
    ) + jnp.einsum(
        "eljic,eljnkc->eljnik", left_rows_im, partner_im, preferred_element_type=jnp.float32
    )
    pair_im = jnp.einsum(
        "eljic,eljnkc->eljnik", left_rows_im, partner_re, preferred_element_type=jnp.float32
    ) - jnp.einsum(
        "eljic,eljnkc->eljnik", left_rows_re, partner_im, preferred_element_type=jnp.float32
    )
    chosen = jnp.stack([pair_re, pair_im], axis=4)
    chosen = chosen.reshape(energy_dev, ATOMS, NBR, 2, NORB, NORB)
    counter = jnp.arange(NORB, dtype=jnp.int32)
    row_mask = counter[None, :] < orbitals[:, None]
    column_mask = counter[None, None, :] < partner_count[:, :, None]
    pair_mask = (row_mask[:, None, :, None] & column_mask[:, :, None, :]).astype(jnp.float32)
    scaled = (
        chosen * occupation[0][:, None, None, None, None, None] * pair_mask[None, :, :, None, :, :]
    )
    pair_blocks = scaled.reshape(energy_dev, ATOMS, NBR, 2, PAIR).astype(jnp.bfloat16)
    arrived = lax.all_to_all(pair_blocks, "shard", split_axis=1, concat_axis=0, tiled=True)
    atom_dev = arrived.shape[1]
    mixed_terms = jnp.einsum(
        "eanpx,anxy->eapy", arrived, coupling, preferred_element_type=jnp.float32
    )
    first_atom = lax.axis_index("shard") * atom_dev
    own_orbitals = lax.dynamic_slice_in_dim(orbitals, first_atom, atom_dev)
    pair_index = jnp.arange(PAIR, dtype=jnp.int32)
    own_mask = (
        (pair_index[None, :] // NORB < own_orbitals[:, None])
        & (pair_index[None, :] % NORB < own_orbitals[:, None])
    ).astype(jnp.float32)
    coupled = (mixed_terms * own_mask[None, :, None, :]).astype(jnp.bfloat16)
    cos_table, sin_table = dft_tables(ENERGIES)
    flat_coupled = coupled.reshape(ENERGIES, -1)
    part_cos = jnp.dot(cos_table, flat_coupled, preferred_element_type=jnp.float32).reshape(
        ENERGIES, atom_dev, 2, PAIR
    )
    part_sin = jnp.dot(sin_table, flat_coupled, preferred_element_type=jnp.float32).reshape(
        ENERGIES, atom_dev, 2, PAIR
    )
    time_data = jnp.stack(
        [part_cos[:, :, 0] + part_sin[:, :, 1], part_cos[:, :, 1] - part_sin[:, :, 0]], axis=2
    ).astype(jnp.bfloat16)
    own_momentum = lax.axis_index("mom")
    mode_count = phonon.shape[0]
    mode_ids = jnp.arange(mode_count, dtype=jnp.int32)
    own_modes = lax.dynamic_slice_in_dim(mode_table, own_momentum, 1, 0)[0]
    phonon_flat = phonon.reshape(mode_count, -1)
    received = lax.all_gather(time_data[None], "mom", axis=0, tiled=True)
    row_count = received.shape[0]
    one_hot = (own_modes[:, None] == mode_ids[None, :]).astype(jnp.float32)
    kernel = jnp.dot(one_hot, phonon_flat, precision=highest).reshape(row_count, 2, ENERGIES)
    values = received.astype(jnp.float32)
    kernel_re = kernel[:, 0][:, :, None, None]
    kernel_im = kernel[:, 1][:, :, None, None]
    add_re = jnp.sum(kernel_re * values[:, :, :, 0] - kernel_im * values[:, :, :, 1], axis=0)
    add_im = jnp.sum(kernel_re * values[:, :, :, 1] + kernel_im * values[:, :, :, 0], axis=0)
    summed = jnp.stack([add_re, add_im], axis=2)
    convolved = summed.astype(jnp.bfloat16)
    flat_conv = convolved.reshape(ENERGIES, -1)
    back_cos = jnp.dot(cos_table, flat_conv, preferred_element_type=jnp.float32).reshape(
        ENERGIES, atom_dev, 2, PAIR
    )
    back_sin = jnp.dot(sin_table, flat_conv, preferred_element_type=jnp.float32).reshape(
        ENERGIES, atom_dev, 2, PAIR
    )
    result_re = (back_cos[:, :, 0] - back_sin[:, :, 1]) * (1.0 / ENERGIES)
    result_im = (back_cos[:, :, 1] + back_sin[:, :, 0]) * (1.0 / ENERGIES)
    return jnp.stack([result_re, result_im], axis=2)[None].astype(jnp.bfloat16)


def solution(mesh):
    in_specs = (
        P("mom", "shard", None, None, None, None),
        P(),
        P("mom", "shard"),
        P(),
        P(),
        P("shard", None, None, None),
        P(),
        P(),
    )
    out_specs = P("mom", None, "shard", None, None)
    return jax.shard_map(local, mesh=mesh, in_specs=in_specs, out_specs=out_specs, check_vma=False)
```

profile of v0, /device:TPU:1, one launch (start us, length us, event | category | flops | bytes accessed | tf_op | source)
XLA Modules:
  0.0 441.8 jit_solution(16534719679795393360)
XLA Ops:
  10.8 10.2 %fusion.16 = bf16[16,8,128,256]{3,2,1,0:T(8,128)(2,1)} fusion(bf16[1,16,8,2,128,128]{5,4,3,2,1,0:T(8,128)(2,1)} %param.8, bf16[1,128,256]{2,1,0:T(8,128)(2,1)S(1)} %get-tuple-element.14, bf16[1,128,256]{2,1,0:T(8,128)(2,1)S(1)} %get-tuple-element.13), kind=kOutput, calls=%fused_computation.19 | convolution fusion | flops 2151940096 | bytes 16908288 | tf_op jit(solution)/shard_map/elpik,pkq->eliq/dot_general | solution.py:36
  21.0 6.1 %fusion.89 = (bf16[16,8,128,128]{3,2,1,0:T(8,128)(2,1)}, bf16[16,8,128,128]{3,2,1,0:T(8,128)(2,1)}) fusion(bf16[16,8,128,256]{3,2,1,0:T(8,128)(2,1)} %fusion.16), kind=kLoop, calls=%fused_computation.125 | loop fusion | bytes 16777216 | tf_op jit(solution)/shard_map/slice | solution.py:51
  27.2 18.0 %convert_bitcast_fusion = bf16[16,8,8,4,2,16,128]{6,2,5,4,0,3,1:T(8,128)(2,1)} fusion(bf16[16,8,2,8,16,128,1]{5,4,3,2,1,0,6:T(8,128)(2,1)} %bitcast.212, s32[8,8,4]{1,2,0:T(4,128)S(1)} %copy.89), kind=kOutput, calls=%fused_computation.2 | convolution fusion | flops 285214720 | bytes 41944064 | tf_op jit(solution)/shard_map/ljnm,elpmic->eljnpic/dot_general | solution.py:45
  45.2 24.1 %slice_bitcast_fusion.1 = (bf16[16,8,8,4,16,128]{5,2,4,0,3,1:T(8,128)(2,1)}, bf16[16,8,8,4,16,128]{5,2,4,0,3,1:T(8,128)(2,1)}) fusion(bf16[16,8,8,4,2,16,128]{6,2,5,4,0,3,1:T(8,128)(2,1)} %convert_bitcast_fusion), kind=kLoop, calls=%fused_computation.4 | loop fusion | bytes 67108864 | tf_op jit(solution)/shard_map/squeeze | solution.py:48
  69.3 17.8 %fusion.2 = f32[16,8,8,4,16,16]{5,4,3,2,1,0:T(8,128)} fusion(bf16[16,8,8,16,128,1]{4,3,5,2,1,0:T(8,128)(2,1)S(1)} %bitcast.209, bf16[16,8,8,4,16,128]{5,2,4,0,3,1:T(8,128)(2,1)} %get-tuple-element.8), kind=kOutput, calls=%fused_computation.8 | convolution fusion | flops 268435456 | bytes 25165824 | tf_op jit(solution)/shard_map/eljic,eljnkc->eljnik/dot_general | solution.py:54
  87.1 17.4 %fusion = f32[16,8,8,4,16,16]{5,4,3,2,1,0:T(8,128)} fusion(bf16[16,8,8,16,128,1]{4,3,5,2,1,0:T(8,128)(2,1)S(1)} %bitcast.211, bf16[16,8,8,4,16,128]{5,2,4,0,3,1:T(8,128)(2,1)} %get-tuple-element.8), kind=kOutput, calls=%fused_computation.6 | convolution fusion | flops 268435456 | bytes 25165824 | tf_op jit(solution)/shard_map/eljic,eljnkc->eljnik/dot_general | solution.py:59
  104.4 28.4 %add_bitcast_fusion = f32[16,8,8,4,16,16]{4,5,3,2,1,0:T(8,128)} fusion(f32[16,8,8,4,16,16]{5,4,3,2,1,0:T(8,128)} %fusion.2, bf16[16,8,8,16,128,1]{4,3,5,2,1,0:T(8,128)(2,1)} %bitcast.210, bf16[16,8,8,4,16,128]{5,2,4,0,3,1:T(8,128)(2,1)} %get-tuple-element.7), kind=kOutput, calls=%fused_computation.1 | convolution fusion | flops 269484032 | bytes 29360128 | tf_op jit(solution)/shard_map/eljic,eljnkc->eljnik/dot_general | solution.py:52
  132.8 32.0 %copy.93 = f32[16,8,8,4,16,16]{5,4,2,1,3,0:T(8,128)} copy(f32[16,8,8,4,16,16]{4,5,3,2,1,0:T(8,128)} %add_bitcast_fusion) | data formatting | bytes 8388608 | tf_op jit(solution)/shard_map/add | solution.py:52
  164.8 23.5 %stack.51 = f32[16,64,4,1,256]{4,1,2,0,3:T(8,128)} reshape(f32[16,8,8,4,16,16]{5,4,2,1,3,0:T(8,128)} %copy.93) | data formatting | bytes 8388608 | tf_op jit(solution)/shard_map/stack | solution.py:62
  188.3 28.5 %subtract_bitcast_fusion = f32[16,8,8,4,16,16]{4,5,3,2,1,0:T(8,128)} fusion(f32[16,8,8,4,16,16]{5,4,3,2,1,0:T(8,128)} %fusion, bf16[16,8,8,16,128,1]{4,3,5,2,1,0:T(8,128)(2,1)} %bitcast.208, bf16[16,8,8,4,16,128]{5,2,4,0,3,1:T(8,128)(2,1)} %get-tuple-element.7), kind=kOutput, calls=%fused_computation | convolution fusion | flops 269484032 | bytes 29360128 | tf_op jit(solution)/shard_map/eljic,eljnkc->eljnik/dot_general | solution.py:57
  216.8 32.0 %copy.96 = f32[16,8,8,4,16,16]{5,4,2,1,3,0:T(8,128)} copy(f32[16,8,8,4,16,16]{4,5,3,2,1,0:T(8,128)} %subtract_bitcast_fusion) | data formatting | bytes 8388608 | tf_op jit(solution)/shard_map/sub | solution.py:57
  248.8 23.5 %stack.52 = f32[16,64,4,1,256]{4,1,2,0,3:T(8,128)} reshape(f32[16,8,8,4,16,16]{5,4,2,1,3,0:T(8,128)} %copy.96) | data formatting | bytes 8388608 | tf_op jit(solution)/shard_map/stack | solution.py:62
  272.8 4.2 fusion.13
  277.0 5.2 %copy.99 = bf16[16,64,4,2,256]{4,2,0,3,1:T(4,128)(2,1)} copy(bf16[16,64,4,2,256]{4,1,2,0,3:T(8,128)(2,1)S(1)} %fusion.13) | data formatting | bytes 8388608 | tf_op jit(solution)/shard_map/convert_element_type | solution.py:71
  282.2 7.4 %all-to-all-start = ((bf16[16,64,4,2,256]{4,2,0,3,1:T(4,128)(2,1)}), bf16[16,64,4,2,256]{4,2,0,3,1:T(4,128)(2,1)}, u32[]{:S(2)}, u32[]{:S(2)}) async-start(bf16[16,64,4,2,256]{4,2,0,3,1:T(4,128)(2,1)} %copy.99), calls=%async_computation | async-start | bytes 8388608 | tf_op jit(solution)/shard_map/all_to_all | solution.py:72
  290.1 77.7 %all-to-all-done = bf16[16,64,4,2,256]{4,2,0,3,1:T(4,128)(2,1)} async-done(((bf16[16,64,4,2,256]{4,2,0,3,1:T(4,128)(2,1)}), bf16[16,64,4,2,256]{4,2,0,3,1:T(4,128)(2,1)}, u32[]{:S(2)}, u32[]{:S(2)}) %all-to-all-start) | async-done | bytes 4194336 | tf_op jit(solution)/shard_map/all_to_all | solution.py:72
  367.7 3.2 copy.100
  372.9 1.3 fusion.55
  374.2 1.3 fusion.58
  377.4 47.1 %all-gather.2.cloned.1.call-done = bf16[2,256,4,2,256]{4,1,3,2,0:T(8,128)(2,1)} async-done(((bf16[1,256,4,2,256]{4,1,3,2,0:T(8,128)(2,1)}), bf16[2,256,4,2,256]{4,1,3,2,0:T(8,128)(2,1)}) %all-gather.2.cloned.1.call-update) | async-done | bytes 2097168 | tf_op jit(solution)/shard_map/all_gather | solution.py:101
  424.5 2.0 convert_element_type.93
  428.3 1.5 copy.107
  429.8 1.4 fusion.35
  432.9 2.0 copy.111
  (60 shorter events, 12.4 us)
Async XLA Ops:
  6.5 365.0 %copy-start = (bf16[4,4,256,256]{3,2,1,0:T(8,128)(2,1)S(1)}, bf16[4,4,256,256]{3,2,1,0:T(8,128)(2,1)}, u32[]{:S(2)}) copy-start(bf16[4,4,256,256]{3,2,1,0:T(8,128)(2,1)} %param.13) | copy-start | bytes 6291460
  21.0 6.1 %copy-start.8 = (s32[64,4]{0,1:T(4,128)S(1)}, s32[64,4]{0,1:T(4,128)}, u32[]{:S(2)}) copy-start(s32[64,4]{0,1:T(4,128)} %param.11) | copy-start | bytes 3076
  27.1 18.1 %copy-start.3 = (s32[64,4]{0,1:T(4,128)}, s32[64,4]{0,1:T(4,128)S(1)}, u32[]{:S(2)}) copy-start(s32[64,4]{0,1:T(4,128)S(1)} %add_select_fusion.1) | copy-start | bytes 3076
  45.2 24.1 %copy-start.1 = (bf16[16,8,128,128]{3,2,1,0:T(8,128)(2,1)S(1)}, bf16[16,8,128,128]{3,2,1,0:T(8,128)(2,1)}, u32[]{:S(2)}) copy-start(bf16[16,8,128,128]{3,2,1,0:T(8,128)(2,1)} %get-tuple-element.9) | copy-start | bytes 12582916
  69.3 17.8 %copy-start.2 = (bf16[16,8,128,128]{3,2,1,0:T(8,128)(2,1)S(1)}, bf16[16,8,128,128]{3,2,1,0:T(8,128)(2,1)}, u32[]{:S(2)}) copy-start(bf16[16,8,128,128]{3,2,1,0:T(8,128)(2,1)} %get-tuple-element.10) | copy-start | bytes 12582916
  248.8 23.5 %copy-start.5 = (s32[8,8]{1,0:T(8,128)S(1)}, s32[8,8]{1,0:T(8,128)}, u32[]{:S(2)}) copy-start(s32[8,8]{1,0:T(8,128)} %reshape.247) | copy-start | bytes 772
  248.8 23.7 %copy-start.4 = (s32[64,4]{0,1:T(4,128)S(1)}, s32[64,4]{0,1:T(4,128)}, u32[]{:S(2)}) copy-start(s32[64,4]{0,1:T(4,128)} %copy-done.3) | copy-start | bytes 3076
  248.8 23.8 %copy-start.6 = (pred[64,16]{0,1:T(8,128)(4,1)S(1)}, pred[64,16]{0,1:T(8,128)(4,1)}, u32[]{:S(2)}) copy-start(pred[64,16]{0,1:T(8,128)(4,1)} %iota_compare_fusion.3) | copy-start | bytes 3076
  248.8 24.1 %copy-start.9 = (f32[1,16]{1,0:T(1,128)S(1)}, f32[1,16]{1,0:T(1,128)}, u32[]{:S(2)}) copy-start(f32[1,16]{1,0:T(1,128)} %param.10) | copy-start | bytes 196
  282.2 7.7 %copy-start.7 = (s32[64]{0:T(128)S(1)}, s32[64]{0:T(128)}, u32[]{:S(2)}) copy-start(s32[64]{0:T(128)} %param.12) | copy-start | bytes 772
  282.2 85.5 %all-to-all-start = ((bf16[16,64,4,2,256]{4,2,0,3,1:T(4,128)(2,1)}), bf16[16,64,4,2,256]{4,2,0,3,1:T(4,128)(2,1)}, u32[]{:S(2)}, u32[]{:S(2)}) async-start(bf16[16,64,4,2,256]{4,2,0,3,1:T(4,128)(2,1)} %copy.99), calls=%async_computation | async-start | bytes 8388608 | tf_op jit(solution)/shard_map/all_to_all | solution.py:72
  289.6 134.9 %all-gather.2.cloned.1.call-start = ((), (), s32[]{:S(2)}) async-start(), calls=%async_computation.1 | async-start | bytes 3145728 | tf_op jit(solution)/shard_map/all_gather | solution.py:101
  375.7 1.4 copy-start.11
  375.8 1.4 copy-start.10
Sparse Core Ops, SparseCore 0:
  377.2 47.1 all-gather.1
where the time goes:
time: 445 us; the launch traced here: 442 us
  local copies, waits for them, and re-layouts  158 us (36%)
  matrix products  127 us (29%)
  waiting for transfers between devices  125 us (28%)
  between operations  13.7 us (3%)
  other arithmetic  11 us (2%)
  starting transfers between devices  7.69 us (2%)
    all_to_all x1, waiting for transfers between devices, local(): lax.all_to_all(pair_blocks, 'shard', split_axis=1, concat_axis=0, tiled=T...  77.7 us
    all_gather x1, waiting for transfers between devices, local(): received = lax.all_gather(time_data[None], 'mom', axis=0, tiled=True)  47.1 us
    another operation x2, local copies, waits for them, and re-layouts, local(): chosen = jnp.stack([pair_re, pair_im], axis=4)  47 us
    sub x1, local copies, waits for them, and re-layouts, local(): jnp.einsum('eljic,eljnkc->eljnik', left_rows_im, partner_re, preferred_el...  32 us
    add x1, local copies, waits for them, and re-layouts, local(): jnp.einsum('eljic,eljnkc->eljnik', left_rows_re, partner_re, preferred_el...  32 us
    dot_general x1, matrix products, local(): jnp.einsum('eljic,eljnkc->eljnik', left_rows_im, partner_re, preferred_el...  28.5 us
    dot_general x1, matrix products, local(): jnp.einsum('eljic,eljnkc->eljnik', left_rows_re, partner_re, preferred_el...  28.4 us
    squeeze x1, local copies, waits for them, and re-layouts, local(): partner_re = partner_rows[:, :, :, :, 0]  24.1 us
  transfers between devices with their start and end apart: 2, of which 2 were waited for; matrix products, arithmetic and copies ran while one was open for 0% of the time, Pallas kernels for 0%

commit v1 on v0

--- a/solution.py
+++ b/solution.py
@@ -1,8 +1,11 @@
+import functools
 import math
 
 import jax
 import jax.numpy as jnp
 from jax import lax
+from jax.experimental import pallas as pl
+from jax.experimental.pallas import tpu as pltpu
 from jax.sharding import PartitionSpec as P
 
 NORB = 16
@@ -121,6 +124,389 @@
     return jnp.stack([result_re, result_im], axis=2)[None].astype(jnp.bfloat16)
 
 
+MESH = pl.DeviceIdType.MESH
+
+
+def phase_plan(atom_dev):
+    if atom_dev < 4:
+        return [(start, 1) for start in range(atom_dev)]
+    first = atom_dev // 2
+    return [(0, first)] + [(start, 1) for start in range(first, atom_dev)]
+
+
+def fused_kernel(
+    phases,
+    shard_count,
+    mom_count,
+    green_hbm,
+    mixing_ref,
+    occ_ref,
+    target_ref,
+    coupling_hbm,
+    phonon_ref,
+    cos_ref,
+    sin_ref,
+    out_ref,
+    green_buf,
+    full_buf,
+    send_buf,
+    recv_buf,
+    coupling_buf,
+    time_buf,
+    green_sem,
+    coupling_sem,
+    own_sem,
+    send_sem,
+    recv_sem,
+    mom_send_sem,
+    mom_recv_sem,
+):
+    me = lax.axis_index("shard")
+    mom = lax.axis_index("mom")
+    layers, energy_dev = green_buf.shape[0], green_buf.shape[1]
+    atom_dev = recv_buf.shape[0]
+    dev_layer = ATL // atom_dev
+    half = layers // 2
+    pieces = NORB // 2
+    last = len(phases) - 1
+
+    def layer_at(step):
+        home = lax.div(me, dev_layer)
+        side = lax.rem(lax.div(home, half) + 1 + lax.div(step, half), 2)
+        return side * half + lax.rem(home + step, half)
+
+    def green_copy(layer):
+        return pltpu.make_async_copy(
+            green_hbm.at[:, layer], green_buf.at[layer], green_sem.at[layer]
+        )
+
+    def coupling_copy():
+        return pltpu.make_async_copy(coupling_hbm, coupling_buf, coupling_sem)
+
+    def own_copy(phase):
+        start, size = phases[phase]
+        return pltpu.make_async_copy(
+            send_buf.at[pl.ds(me * atom_dev + start, size)],
+            recv_buf.at[pl.ds(start, size), :, me],
+            own_sem.at[phase],
+        )
+
+    def send_copy(phase, dest):
+        start, size = phases[phase]
+        return pltpu.make_async_remote_copy(
+            src_ref=send_buf.at[pl.ds(dest * atom_dev + start, size)],
+            dst_ref=recv_buf.at[pl.ds(start, size), :, me],
+            send_sem=send_sem.at[phase, dest],
+            recv_sem=recv_sem.at[phase, me],
+            device_id={"shard": dest},
+            device_id_type=MESH,
+        )
+
+    def arrive_copy(phase, source):
+        start, size = phases[phase]
+        return pltpu.make_async_remote_copy(
+            src_ref=send_buf.at[pl.ds(source * atom_dev + start, size)],
+            dst_ref=recv_buf.at[pl.ds(start, size), :, source],
+            send_sem=send_sem.at[phase, source],
+            recv_sem=recv_sem.at[phase, source],
+            device_id={"shard": source},
+            device_id_type=MESH,
+        )
+
+    def mom_copy(phase, step, sending):
+        start, size = phases[phase]
+        dest = lax.rem(mom + step, mom_count)
+        source = lax.rem(mom + mom_count - step, mom_count)
+        origin = mom if sending else source
+        return pltpu.make_async_remote_copy(
+            src_ref=time_buf.at[mom, pl.ds(start, size)],
+            dst_ref=time_buf.at[origin, pl.ds(start, size)],
+            send_sem=mom_send_sem.at[phase, step - 1],
+            recv_sem=mom_recv_sem.at[phase, step - 1],
+            device_id={"mom": dest},
+            device_id_type=MESH,
+        )
+
+    for step in range(layers):
+        green_copy(layer_at(step)).start()
+    coupling_copy().start()
+
+    barrier = pltpu.get_barrier_semaphore()
+    for step in range(1, shard_count):
+        pl.semaphore_signal(
+            barrier,
+            inc=1,
+            device_id={"shard": lax.rem(me + step, shard_count)},
+            device_id_type=MESH,
+        )
+    for step in range(1, mom_count):
+        pl.semaphore_signal(
+            barrier,
+            inc=1,
+            device_id={"mom": lax.rem(mom + step, mom_count)},
+            device_id_type=MESH,
+        )
+    pl.semaphore_wait(barrier, shard_count + mom_count - 2)
+
+    group = 4 if energy_dev % 4 == 0 else 1
+
+    def layer_step(step, carry):
+        layer = layer_at(step)
+        green_copy(layer).wait()
+
+        def energy_step(index, inner):
+            first = index * group
+            joined = [
+                jnp.concatenate(
+                    [green_buf[layer, first + j, 0], green_buf[layer, first + j, 1]], axis=1
+                )
+                for j in range(group)
+            ]
+            left = jnp.dot(
+                jnp.concatenate(joined, axis=0),
+                mixing_ref[...],
+                preferred_element_type=jnp.float32,
+            ).astype(jnp.bfloat16)
+            for j in range(group):
+                turned = jnp.concatenate(
+                    [-joined[j][:, ORB:], joined[j][:, :ORB]], axis=1
+                )
+                full = lax.dot_general(
+                    left[j * ORB : (j + 1) * ORB],
+                    jnp.concatenate([joined[j], turned], axis=0),
+                    (((1,), (1,)), ((), ())),
+                    preferred_element_type=jnp.float32,
+                )
+                rows = pl.ds(pl.multiple_of((first + j) * ORB, ORB), ORB)
+                full_buf[0, rows, :] = full[:, :ORB]
+                full_buf[1, rows, :] = full[:, ORB:]
+            return inner
+
+        lax.fori_loop(0, energy_dev // group, energy_step, 0)
+
+        def atom_step(slot, inner):
+            atom = layer * ATL + slot
+            weight = occ_ref[...]
+            strips = []
+            for part in range(2):
+                for piece in range(pieces):
+                    pair = [
+                        (
+                            full_buf[
+                                part,
+                                pl.ds(slot * NORB + 2 * piece + low, energy_dev, stride=ORB),
+                                :,
+                            ]
+                            * weight
+                        ).astype(jnp.bfloat16)
+                        for low in range(2)
+                    ]
+                    strips.append(jnp.concatenate(pair, axis=1))
+            stacked = jnp.concatenate(strips, axis=0)
+            row_ids = lax.broadcasted_iota(jnp.int32, (2 * ORB, ORB), 0)
+            chosen = jnp.where(row_ids == target_ref[pl.ds(atom, 1), :], 1.0, 0.0)
+            picked = jnp.dot(
+                stacked, chosen.astype(jnp.bfloat16), preferred_element_type=jnp.float32
+            )
+            send_buf[atom] = picked.astype(jnp.bfloat16).reshape(2 * pieces, energy_dev, ORB)
+            return inner
+
+        lax.fori_loop(0, ATL, atom_step, 0)
+        start_sends(0, layer)
+        return carry
+
+    def start_sends(phase, layer):
+        for offset in range(dev_layer):
+            dest = layer * dev_layer + offset
+
+            @pl.when(dest != me)
+            def _():
+                if phase > 0:
+                    send_copy(phase - 1, dest).wait_send()
+                send_copy(phase, dest).start()
+
+            @pl.when(dest == me)
+            def _():
+                own_copy(phase).start()
+
+    def finish(phase):
+        start, size = phases[phase]
+        for step in range(1, mom_count):
+            mom_copy(phase, step, False).wait_recv()
+        for atom in range(start, start + size):
+            sums = [0.0, 0.0]
+            for other in range(mom_count):
+                wide_re = jnp.concatenate([phonon_ref[other, 0]] * (PAIR // ORB), axis=1)
+                wide_im = jnp.concatenate([phonon_ref[other, 1]] * (PAIR // ORB), axis=1)
+                time_re = time_buf[other, atom, 0].astype(jnp.float32)
+                time_im = time_buf[other, atom, 1].astype(jnp.float32)
+                sums[0] = sums[0] + (wide_re * time_re - wide_im * time_im)
+                sums[1] = sums[1] + (wide_re * time_im + wide_im * time_re)
+            conv_re = sums[0].astype(jnp.bfloat16)
+            conv_im = sums[1].astype(jnp.bfloat16)
+            dot = functools.partial(jnp.dot, preferred_element_type=jnp.float32)
+            scale = 1.0 / cos_ref.shape[0]
+            res_re = (dot(cos_ref[...], conv_re) - dot(sin_ref[...], conv_im)) * scale
+            res_im = (dot(cos_ref[...], conv_im) + dot(sin_ref[...], conv_re)) * scale
+            base = atom * 2 * PAIR
+            out_ref[:, base : base + PAIR] = res_re.astype(jnp.bfloat16)
+            out_ref[:, base + PAIR : base + 2 * PAIR] = res_im.astype(jnp.bfloat16)
+
+    def transform(phase):
+        start, size = phases[phase]
+
+        def arrive(source, carry):
+            @pl.when(source != me)
+            def _():
+                arrive_copy(phase, source).wait_recv()
+
+            return carry
+
+        lax.fori_loop(0, shard_count, arrive, 0)
+        own_copy(phase).wait()
+        energies = shard_count * energy_dev
+        for atom in range(start, start + size):
+            coupled = []
+            for part in range(2):
+                total = 0.0
+                for piece in range(0, pieces, 2):
+                    block = jnp.concatenate(
+                        [
+                            recv_buf[atom, part * pieces + piece + low].reshape(energies, ORB)
+                            for low in range(2)
+                        ],
+                        axis=1,
+                    )
+                    total = total + jnp.dot(
+                        block,
+                        coupling_buf[atom, piece * ORB : (piece + 2) * ORB, :],
+                        preferred_element_type=jnp.float32,
+                    )
+                coupled.append(total.astype(jnp.bfloat16))
+            dot = functools.partial(jnp.dot, preferred_element_type=jnp.float32)
+            time_re = dot(cos_ref[...], coupled[0]) + dot(sin_ref[...], coupled[1])
+            time_im = dot(cos_ref[...], coupled[1]) - dot(sin_ref[...], coupled[0])
+            time_buf[mom, atom, 0] = time_re.astype(jnp.bfloat16)
+            time_buf[mom, atom, 1] = time_im.astype(jnp.bfloat16)
+        for step in range(1, mom_count):
+            mom_copy(phase, step, True).start()
+
+    lax.fori_loop(0, layers, layer_step, 0)
+    coupling_copy().wait()
+    for phase in range(len(phases)):
+        if phase < last:
+
+            def more(step, carry):
+                start_sends(phase + 1, layer_at(step))
+                return carry
+
+            lax.fori_loop(0, layers, more, 0)
+        transform(phase)
+        if phase > 0:
+            finish(phase - 1)
+    finish(last)
+
+    def drain(dest, carry):
+        @pl.when(dest != me)
+        def _():
+            send_copy(last, dest).wait_send()
+
+        return carry
+
+    lax.fori_loop(0, shard_count, drain, 0)
+    for phase in range(len(phases)):
+        for step in range(1, mom_count):
+            mom_copy(phase, step, True).wait_send()
+
+
+def fused(shard_count, mom_count, green_ret, broadening, occupation, neighbours, orbitals,
+          coupling, phonon, mode_table):
+    greens = green_ret[0]
+    energy_dev = greens.shape[0]
+    atom_dev = coupling.shape[0]
+    energies = phonon.shape[-1]
+    mixing = jnp.concatenate(
+        [
+            jnp.concatenate([broadening[0], broadening[1]], axis=1),
+            jnp.concatenate([-broadening[1], broadening[0]], axis=1),
+        ],
+        axis=0,
+    )
+    occ = jnp.broadcast_to(occupation[0][:, None], (energy_dev, ORB))
+    lane = jnp.arange(ORB, dtype=jnp.int32)
+    slots = neighbours % ATL
+    lane_slot = lane // NORB % NBR
+    lane_atom = jnp.sum(
+        jnp.where(lane_slot[None, None, :] == jnp.arange(NBR)[None, :, None], slots[:, :, None], 0),
+        axis=1,
+    )
+    target = lane_atom * NORB + (lane % NORB + lane // (NORB * NBR) * ORB)[None, :]
+    first_atom = lax.axis_index("shard") * atom_dev
+    own_orbitals = lax.dynamic_slice_in_dim(orbitals, first_atom, atom_dev)
+    own_neighbours = lax.dynamic_slice_in_dim(neighbours, first_atom, atom_dev)
+    partner = jnp.sum(
+        jnp.where(
+            own_neighbours[:, :, None] == jnp.arange(ATOMS, dtype=jnp.int32)[None, None, :],
+            orbitals[None, None, :],
+            0,
+        ),
+        axis=2,
+    )
+    counter = jnp.arange(NORB, dtype=jnp.int32)
+    within = counter[None, :] < own_orbitals[:, None]
+    column = counter[None, None, :] < partner[:, :, None]
+    pair_index = jnp.arange(PAIR, dtype=jnp.int32)
+    final = (pair_index[None, :] // NORB < own_orbitals[:, None]) & (
+        pair_index[None, :] % NORB < own_orbitals[:, None]
+    )
+    keep = (
+        within[:, :, None, None, None]
+        & column[:, None, :, :, None]
+        & final[:, None, None, None, :]
+    )
+    ordered = coupling.reshape(atom_dev, NBR, NORB, NORB, PAIR).transpose(0, 2, 1, 3, 4)
+    ordered = jnp.where(keep, ordered, jnp.zeros((), coupling.dtype))
+    ordered = ordered.reshape(atom_dev, NBR * PAIR, PAIR)
+    modes = lax.dynamic_slice_in_dim(mode_table, lax.axis_index("mom"), 1, 0)[0]
+    mode_ids = jnp.arange(phonon.shape[0], dtype=jnp.int32)
+    kernels = jnp.sum(
+        jnp.where((modes[:, None] == mode_ids[None, :])[:, :, None, None], phonon[None], 0.0),
+        axis=1,
+    )
+    kernels = jnp.broadcast_to(kernels[..., None], kernels.shape + (ORB,))
+    cos_table, sin_table = dft_tables(energies)
+    phases = phase_plan(atom_dev)
+    count = len(phases)
+    vmem = pl.BlockSpec(memory_space=pltpu.VMEM)
+    hbm = pl.BlockSpec(memory_space=pl.ANY)
+    dma = pltpu.SemaphoreType.DMA
+    result = pl.pallas_call(
+        functools.partial(fused_kernel, phases, shard_count, mom_count),
+        out_shape=jax.ShapeDtypeStruct((energies, atom_dev * 2 * PAIR), jnp.bfloat16),
+        in_specs=[hbm, vmem, vmem, vmem, hbm, vmem, vmem, vmem],
+        out_specs=vmem,
+        scratch_shapes=[
+            pltpu.VMEM((LAYERS, energy_dev, 2, ORB, ORB), jnp.bfloat16),
+            pltpu.VMEM((2, energy_dev * ORB, ORB), jnp.float32),
+            pltpu.VMEM((ATOMS, NORB, energy_dev, ORB), jnp.bfloat16),
+            pltpu.VMEM((atom_dev, NORB, shard_count, energy_dev, ORB), jnp.bfloat16),
+            pltpu.VMEM((atom_dev, NBR * PAIR, PAIR), jnp.bfloat16),
+            pltpu.VMEM((mom_count, atom_dev, 2, energies, PAIR), jnp.bfloat16),
+            dma((LAYERS,)),
+            dma,
+            dma((count,)),
+            dma((count, shard_count)),
+            dma((count, shard_count)),
+            dma((count, max(mom_count - 1, 1))),
+            dma((count, max(mom_count - 1, 1))),
+        ],
+        compiler_params=pltpu.CompilerParams(
+            collective_id=0, has_side_effects=True, vmem_limit_bytes=48 * 1024 * 1024
+        ),
+    )(greens, mixing, occ, target, ordered, kernels, cos_table, sin_table)
+    return result.reshape(1, energies, atom_dev, 2, PAIR)
+
+
 def solution(mesh):
     in_specs = (
         P("mom", "shard", None, None, None, None),
@@ -133,4 +519,12 @@
         P(),
     )
     out_specs = P("mom", None, "shard", None, None)
-    return jax.shard_map(local, mesh=mesh, in_specs=in_specs, out_specs=out_specs, check_vma=False)
+    shard_count, mom_count = mesh.shape["shard"], mesh.shape["mom"]
+
+    def body(*args):
+        energy_dev, atom_dev = args[0].shape[1], args[5].shape[0]
+        if energy_dev % 16 == 0 and ATL % atom_dev == 0:
+            return fused(shard_count, mom_count, *args)
+        return local(*args)
+
+    return jax.shard_map(body, mesh=mesh, in_specs=in_specs, out_specs=out_specs, check_vma=False)

time: 445 us -> 125 us (0.28)
  local copies, waits for them, and re-layouts: 158 us -> 6.26 us
  matrix products: 127 us -> 0 us
  waiting for transfers between devices: 125 us -> 0 us
  Pallas kernels: 0 us -> 112 us
  between operations: 13.7 us -> 0.07 us
  starting transfers between devices: 7.69 us -> 0 us
  other arithmetic: 11 us -> 6.24 us
    dot_general x12 -> x0, matrix products: 127 us -> none  [the longest x1 28.5 us: local(): jnp.einsum('eljic,eljnkc->eljnik', left_rows_im, partner_re, preferred_el...]
    pallas_call x0 -> x1, Pallas kernels: none -> 112 us  [fused(): pl.pallas_call(functools.partial(fused_kernel, phases, shard_count, mom_c...]
    all_to_all x1 -> x0, waiting for transfers between devices: 77.7 us -> none  [local(): lax.all_to_all(pair_blocks, 'shard', split_axis=1, concat_axis=0, tiled=T...]
    another operation x5 -> x0, local copies, waits for them, and re-layouts: 51.6 us -> none  [the longest x2 47 us: local(): chosen = jnp.stack([pair_re, pair_im], axis=4)]
    all_gather x1 -> x0, waiting for transfers between devices: 47.1 us -> none  [local(): received = lax.all_gather(time_data[None], 'mom', axis=0, tiled=True)]
    sub x1 -> x0, local copies, waits for them, and re-layouts: 32 us -> none  [local(): jnp.einsum('eljic,eljnkc->eljnik', left_rows_im, partner_re, preferred_el...]
    add x1 -> x0, local copies, waits for them, and re-layouts: 32 us -> none  [local(): jnp.einsum('eljic,eljnkc->eljnik', left_rows_re, partner_re, preferred_el...]
    squeeze x2 -> x1, local copies, waits for them, and re-layouts: 25 us -> 0.78 us  [fused(): broadening[1]]
  transfers between devices with their start and end apart: 2 -> 0, of which waited for: 2 -> 0; matrix products, arithmetic and copies ran while one was open for 0% -> 0% of each run, Pallas kernels for 0% -> 0%
where the time goes in v1:
time: 125 us
  Pallas kernels  112 us (90%)
  local copies, waits for them, and re-layouts  6.26 us (5%)
  other arithmetic  6.24 us (5%)
    pallas_call x1, Pallas kernels, fused(): pl.pallas_call(functools.partial(fused_kernel, phases, shard_count, mom_c...  112 us

profile of v1, /device:TPU:1, one launch (start us, length us, event | category | flops | bytes accessed | tf_op | source)
XLA Modules:
  0.0 124.5 jit_solution(4169483879690222788)
XLA Ops:
  0.0 0.0 copy-start
  0.0 0.7 copy-done
  0.7 0.1 iota_compare_fusion.4
  0.8 0.7 dynamic_slice.9
  1.5 0.1 iota_compare_fusion.2
  1.6 0.8 constant_dynamic-slice_fusion
  2.3 0.1 copy.12
  2.4 0.9 select_reduce_fusion.2
  3.3 0.1 iota_compare_fusion.1
  3.4 0.7 add_select_fusion.1
  4.1 0.1 compare_and_fusion
  4.2 0.7 broadcast_in_dim.63.occ_ref
  4.9 0.7 copy.14
  5.6 0.1 select_reduce_fusion.1
  5.7 0.1 select_reduce_fusion
  5.8 0.1 broadcast_and_fusion
  6.0 0.8 fusion.12
  6.7 0.8 slice_bitcast_fusion
  7.5 1.1 sine_convert_fusion
  8.6 0.2 broadcast_in_dim.103.phonon_ref
  8.8 2.1 %and_select_fusion = bf16[4,16,4,16,256]{4,3,2,1,0:T(8,128)(2,1)S(1)} fusion(bf16[4,4,16,16,256]{4,3,2,1,0:T(8,128)(2,1)} %bitcast.16, pred[4,256]{1,0:T(4,128)(4,1)S(1)} %compare_and_fusion, pred[4,16,4,16]{3,2,1,0:T(4,128)(4,1)S(1)} %broadcast_and_fusion), kind=kLoop, calls=%fused_computation | loop fusion | flops 2097152 | bytes 4199424 | tf_op jit(solution)/shard_map/jit(_where)/select_n | solution.py:468
  11.0 111.9 %shard_map.82 = bf16[256,2048]{1,0:T(8,128)(2,1)S(1)} custom-call(bf16[16,8,2,128,128]{4,3,2,1,0:T(8,128)(2,1)} %bitcast.15, bf16[256,256]{1,0:T(8,128)(2,1)S(1)} %maximum_maximum_fusion.mixing_ref, f32[16,128]{1,0:T(8,128)S(1)} %broadcast_in_dim.63.occ_ref, s32[64,128]{1,0:T(8,128)S(1)} %multiply_add_fusion.target_ref, bf16[4,1024,256]{2,1,0:T(8,128)(2,1)S(1)} %bitcast.14, ...), custom_call_target="tpu_custom_call" | custom-call | tf_op jit(solution)/shard_map/pallas_call | solution.py:483
  122.9 1.6 %reshape.237 = bf16[1,256,4,2,256]{4,3,2,1,0:T(2,128)(2,1)} reshape(bf16[256,2048]{1,0:T(8,128)(2,1)S(1)} %shard_map.82) | data formatting | bytes 2097152 | tf_op jit(solution)/shard_map/reshape | solution.py:507
  (6 shorter events, 0.0 us)
Async XLA Ops:
  0.0 0.7 copy-start

commit v2 on v1

--- a/solution.py
+++ b/solution.py
@@ -3,6 +3,7 @@
 
 import jax
 import jax.numpy as jnp
+import numpy as np
 from jax import lax
 from jax.experimental import pallas as pl
 from jax.experimental.pallas import tpu as pltpu
@@ -128,10 +129,9 @@
 
 
 def phase_plan(atom_dev):
-    if atom_dev < 4:
-        return [(start, 1) for start in range(atom_dev)]
-    first = atom_dev // 2
-    return [(0, first)] + [(start, 1) for start in range(first, atom_dev)]
+    if atom_dev < 2:
+        return [(0, atom_dev)]
+    return [(0, atom_dev - 1), (atom_dev - 1, 1)]
 
 
 def fused_kernel(
@@ -139,11 +139,13 @@
     shard_count,
     mom_count,
     green_hbm,
-    mixing_ref,
-    occ_ref,
-    target_ref,
+    broadening_ref,
+    occupation_ref,
+    neighbours_ref,
+    orbitals_ref,
     coupling_hbm,
     phonon_ref,
+    modes_ref,
     cos_ref,
     sin_ref,
     out_ref,
@@ -152,6 +154,8 @@
     send_buf,
     recv_buf,
     coupling_buf,
+    kernel_buf,
+    mixing_ref,
     time_buf,
     green_sem,
     coupling_sem,
@@ -180,14 +184,16 @@
             green_hbm.at[:, layer], green_buf.at[layer], green_sem.at[layer]
         )
 
-    def coupling_copy():
-        return pltpu.make_async_copy(coupling_hbm, coupling_buf, coupling_sem)
+    def coupling_copy(slot):
+        return pltpu.make_async_copy(
+            coupling_hbm.at[:, slot], coupling_buf.at[:, :, slot], coupling_sem.at[slot]
+        )
 
     def own_copy(phase):
         start, size = phases[phase]
         return pltpu.make_async_copy(
             send_buf.at[pl.ds(me * atom_dev + start, size)],
-            recv_buf.at[pl.ds(start, size), :, me],
+            recv_buf.at[pl.ds(start, size), me],
             own_sem.at[phase],
         )
 
@@ -195,7 +201,7 @@
         start, size = phases[phase]
         return pltpu.make_async_remote_copy(
             src_ref=send_buf.at[pl.ds(dest * atom_dev + start, size)],
-            dst_ref=recv_buf.at[pl.ds(start, size), :, me],
+            dst_ref=recv_buf.at[pl.ds(start, size), me],
             send_sem=send_sem.at[phase, dest],
             recv_sem=recv_sem.at[phase, me],
             device_id={"shard": dest},
@@ -206,7 +212,7 @@
         start, size = phases[phase]
         return pltpu.make_async_remote_copy(
             src_ref=send_buf.at[pl.ds(source * atom_dev + start, size)],
-            dst_ref=recv_buf.at[pl.ds(start, size), :, source],
+            dst_ref=recv_buf.at[pl.ds(start, size), source],
             send_sem=send_sem.at[phase, source],
             recv_sem=recv_sem.at[phase, source],
             device_id={"shard": source},
@@ -229,7 +235,8 @@
 
     for step in range(layers):
         green_copy(layer_at(step)).start()
-    coupling_copy().start()
+    for slot in range(NBR):
+        coupling_copy(slot).start()
 
     barrier = pltpu.get_barrier_semaphore()
     for step in range(1, shard_count):
@@ -246,12 +253,14 @@
             device_id={"mom": lax.rem(mom + step, mom_count)},
             device_id_type=MESH,
         )
-    pl.semaphore_wait(barrier, shard_count + mom_count - 2)
-
-    group = 4 if energy_dev % 4 == 0 else 1
-
-    def layer_step(step, carry):
-        layer = layer_at(step)
+    mixing_ref[:ORB, :ORB] = broadening_ref[0]
+    mixing_ref[:ORB, ORB:] = broadening_ref[1]
+    mixing_ref[ORB:, :ORB] = -broadening_ref[1]
+    mixing_ref[ORB:, ORB:] = broadening_ref[0]
+    group = 8
+    unroll = 4
+
+    def layer_pairs(layer):
         green_copy(layer).wait()
 
         def energy_step(index, inner):
@@ -277,6 +286,7 @@
                     (((1,), (1,)), ((), ())),
                     preferred_element_type=jnp.float32,
                 )
+                full = full * occupation_ref[0, first + j]
                 rows = pl.ds(pl.multiple_of((first + j) * ORB, ORB), ORB)
                 full_buf[0, rows, :] = full[:, :ORB]
                 full_buf[1, rows, :] = full[:, ORB:]
@@ -284,36 +294,82 @@
 
         lax.fori_loop(0, energy_dev // group, energy_step, 0)
 
-        def atom_step(slot, inner):
+        lane = lax.broadcasted_iota(jnp.int32, (1, ORB), 1)
+        lane_slot = lax.rem(lax.div(lane, NORB), NBR)
+        lane_base = lax.rem(lane, NORB) + lax.div(lane, NORB * NBR) * ORB
+        row_ids = lax.broadcasted_iota(jnp.int32, (2 * ORB, ORB), 0)
+
+        def pick_atom(slot):
             atom = layer * ATL + slot
-            weight = occ_ref[...]
+            target = lane_base
+            for near in range(NBR):
+                start = (neighbours_ref[atom, near] - layer * ATL) * NORB
+                target = target + jnp.where(lane_slot == near, start, 0)
             strips = []
             for part in range(2):
                 for piece in range(pieces):
                     pair = [
-                        (
-                            full_buf[
-                                part,
-                                pl.ds(slot * NORB + 2 * piece + low, energy_dev, stride=ORB),
-                                :,
-                            ]
-                            * weight
-                        ).astype(jnp.bfloat16)
+                        full_buf[
+                            part,
+                            pl.ds(slot * NORB + 2 * piece + low, energy_dev, stride=ORB),
+                            :,
+                        ].astype(jnp.bfloat16)
                         for low in range(2)
                     ]
                     strips.append(jnp.concatenate(pair, axis=1))
             stacked = jnp.concatenate(strips, axis=0)
-            row_ids = lax.broadcasted_iota(jnp.int32, (2 * ORB, ORB), 0)
-            chosen = jnp.where(row_ids == target_ref[pl.ds(atom, 1), :], 1.0, 0.0)
+            chosen = jnp.where(row_ids == target, 1.0, 0.0)
             picked = jnp.dot(
                 stacked, chosen.astype(jnp.bfloat16), preferred_element_type=jnp.float32
             )
             send_buf[atom] = picked.astype(jnp.bfloat16).reshape(2 * pieces, energy_dev, ORB)
+
+        def atom_step(index, inner):
+            for j in range(unroll):
+                pick_atom(index * unroll + j)
             return inner
 
-        lax.fori_loop(0, ATL, atom_step, 0)
-        start_sends(0, layer)
+        lax.fori_loop(0, ATL // unroll, atom_step, 0)
+
+    def layer_step(step, carry):
+        layer_pairs(layer_at(step))
+        start_sends(0, layer_at(step))
         return carry
+
+    def mask_coupling():
+        shape = (NORB, PAIR)
+        column = lax.broadcasted_iota(jnp.int32, shape, 0)
+        entry = lax.broadcasted_iota(jnp.int32, shape, 1)
+        outer, inner = lax.div(entry, NORB), lax.rem(entry, NORB)
+        for slot in range(NBR):
+            coupling_copy(slot).wait()
+        for atom in range(atom_dev):
+            place = me * atom_dev + atom
+            own = orbitals_ref[place]
+            kept = (outer < own) & (inner < own)
+            masks = [
+                jnp.where(kept & (column < orbitals_ref[neighbours_ref[place, near]]), 1.0, 0.0)
+                for near in range(NBR)
+            ]
+
+            def row_step(row, carry):
+                used = jnp.where(row < own, 1.0, 0.0)
+                for near in range(NBR):
+                    block = coupling_buf[atom, row, near].astype(jnp.float32)
+                    coupling_buf[atom, row, near] = (block * (masks[near] * used)).astype(
+                        jnp.bfloat16
+                    )
+                return carry
+
+            lax.fori_loop(0, NORB, row_step, 0)
+
+    def spread_phonon():
+        for other in range(mom_count):
+            mode = modes_ref[mom, other]
+            rows = phonon_ref[mode]
+            for part in range(2):
+                wide = jnp.broadcast_to(rows[part : part + 1], (ORB, rows.shape[1]))
+                kernel_buf[other, part] = wide.T
 
     def start_sends(phase, layer):
         for offset in range(dev_layer):
@@ -336,8 +392,8 @@
         for atom in range(start, start + size):
             sums = [0.0, 0.0]
             for other in range(mom_count):
-                wide_re = jnp.concatenate([phonon_ref[other, 0]] * (PAIR // ORB), axis=1)
-                wide_im = jnp.concatenate([phonon_ref[other, 1]] * (PAIR // ORB), axis=1)
+                wide_re = jnp.concatenate([kernel_buf[other, 0]] * (PAIR // ORB), axis=1)
+                wide_im = jnp.concatenate([kernel_buf[other, 1]] * (PAIR // ORB), axis=1)
                 time_re = time_buf[other, atom, 0].astype(jnp.float32)
                 time_im = time_buf[other, atom, 1].astype(jnp.float32)
                 sums[0] = sums[0] + (wide_re * time_re - wide_im * time_im)
@@ -372,14 +428,14 @@
                 for piece in range(0, pieces, 2):
                     block = jnp.concatenate(
                         [
-                            recv_buf[atom, part * pieces + piece + low].reshape(energies, ORB)
+                            recv_buf[atom, :, part * pieces + piece + low].reshape(energies, ORB)
                             for low in range(2)
                         ],
                         axis=1,
                     )
                     total = total + jnp.dot(
                         block,
-                        coupling_buf[atom, piece * ORB : (piece + 2) * ORB, :],
+                        coupling_buf[atom, 2 * piece : 2 * piece + 4].reshape(PAIR, PAIR),
                         preferred_element_type=jnp.float32,
                     )
                 coupled.append(total.astype(jnp.bfloat16))
@@ -391,8 +447,12 @@
         for step in range(1, mom_count):
             mom_copy(phase, step, True).start()
 
-    lax.fori_loop(0, layers, layer_step, 0)
-    coupling_copy().wait()
+    layer_pairs(layer_at(0))
+    pl.semaphore_wait(barrier, shard_count + mom_count - 2)
+    start_sends(0, layer_at(0))
+    lax.fori_loop(1, layers, layer_step, 0)
+    mask_coupling()
+    spread_phonon()
     for phase in range(len(phases)):
         if phase < last:
 
@@ -425,75 +485,34 @@
     energy_dev = greens.shape[0]
     atom_dev = coupling.shape[0]
     energies = phonon.shape[-1]
-    mixing = jnp.concatenate(
-        [
-            jnp.concatenate([broadening[0], broadening[1]], axis=1),
-            jnp.concatenate([-broadening[1], broadening[0]], axis=1),
-        ],
-        axis=0,
-    )
-    occ = jnp.broadcast_to(occupation[0][:, None], (energy_dev, ORB))
-    lane = jnp.arange(ORB, dtype=jnp.int32)
-    slots = neighbours % ATL
-    lane_slot = lane // NORB % NBR
-    lane_atom = jnp.sum(
-        jnp.where(lane_slot[None, None, :] == jnp.arange(NBR)[None, :, None], slots[:, :, None], 0),
-        axis=1,
-    )
-    target = lane_atom * NORB + (lane % NORB + lane // (NORB * NBR) * ORB)[None, :]
-    first_atom = lax.axis_index("shard") * atom_dev
-    own_orbitals = lax.dynamic_slice_in_dim(orbitals, first_atom, atom_dev)
-    own_neighbours = lax.dynamic_slice_in_dim(neighbours, first_atom, atom_dev)
-    partner = jnp.sum(
-        jnp.where(
-            own_neighbours[:, :, None] == jnp.arange(ATOMS, dtype=jnp.int32)[None, None, :],
-            orbitals[None, None, :],
-            0,
-        ),
-        axis=2,
-    )
-    counter = jnp.arange(NORB, dtype=jnp.int32)
-    within = counter[None, :] < own_orbitals[:, None]
-    column = counter[None, None, :] < partner[:, :, None]
-    pair_index = jnp.arange(PAIR, dtype=jnp.int32)
-    final = (pair_index[None, :] // NORB < own_orbitals[:, None]) & (
-        pair_index[None, :] % NORB < own_orbitals[:, None]
-    )
-    keep = (
-        within[:, :, None, None, None]
-        & column[:, None, :, :, None]
-        & final[:, None, None, None, :]
-    )
-    ordered = coupling.reshape(atom_dev, NBR, NORB, NORB, PAIR).transpose(0, 2, 1, 3, 4)
-    ordered = jnp.where(keep, ordered, jnp.zeros((), coupling.dtype))
-    ordered = ordered.reshape(atom_dev, NBR * PAIR, PAIR)
-    modes = lax.dynamic_slice_in_dim(mode_table, lax.axis_index("mom"), 1, 0)[0]
-    mode_ids = jnp.arange(phonon.shape[0], dtype=jnp.int32)
-    kernels = jnp.sum(
-        jnp.where((modes[:, None] == mode_ids[None, :])[:, :, None, None], phonon[None], 0.0),
-        axis=1,
-    )
-    kernels = jnp.broadcast_to(kernels[..., None], kernels.shape + (ORB,))
-    cos_table, sin_table = dft_tables(energies)
+    counter = np.arange(energies, dtype=np.int32)
+    angles = (counter[:, None] * counter[None, :] % energies).astype(np.float32)
+    angles = angles * np.float32(2.0 * math.pi / energies)
+    cos_table = jnp.asarray(np.cos(angles), jnp.bfloat16)
+    sin_table = jnp.asarray(np.sin(angles), jnp.bfloat16)
+    blocks = coupling.reshape(atom_dev, NBR, NORB, NORB, PAIR)
     phases = phase_plan(atom_dev)
     count = len(phases)
     vmem = pl.BlockSpec(memory_space=pltpu.VMEM)
     hbm = pl.BlockSpec(memory_space=pl.ANY)
+    smem = pl.BlockSpec(memory_space=pltpu.SMEM)
     dma = pltpu.SemaphoreType.DMA
     result = pl.pallas_call(
         functools.partial(fused_kernel, phases, shard_count, mom_count),
         out_shape=jax.ShapeDtypeStruct((energies, atom_dev * 2 * PAIR), jnp.bfloat16),
-        in_specs=[hbm, vmem, vmem, vmem, hbm, vmem, vmem, vmem],
+        in_specs=[hbm, vmem, smem, smem, smem, hbm, vmem, smem, vmem, vmem],
         out_specs=vmem,
         scratch_shapes=[
             pltpu.VMEM((LAYERS, energy_dev, 2, ORB, ORB), jnp.bfloat16),
             pltpu.VMEM((2, energy_dev * ORB, ORB), jnp.float32),
             pltpu.VMEM((ATOMS, NORB, energy_dev, ORB), jnp.bfloat16),
-            pltpu.VMEM((atom_dev, NORB, shard_count, energy_dev, ORB), jnp.bfloat16),
-            pltpu.VMEM((atom_dev, NBR * PAIR, PAIR), jnp.bfloat16),
+            pltpu.VMEM((atom_dev, shard_count, NORB, energy_dev, ORB), jnp.bfloat16),
+            pltpu.VMEM((atom_dev, NORB, NBR, NORB, PAIR), jnp.bfloat16),
+            pltpu.VMEM((mom_count, 2, energies, ORB), jnp.float32),
+            pltpu.VMEM((2 * ORB, 2 * ORB), jnp.bfloat16),
             pltpu.VMEM((mom_count, atom_dev, 2, energies, PAIR), jnp.bfloat16),
             dma((LAYERS,)),
-            dma,
+            dma((NBR,)),
             dma((count,)),
             dma((count, shard_count)),
             dma((count, shard_count)),
@@ -503,7 +522,10 @@
         compiler_params=pltpu.CompilerParams(
             collective_id=0, has_side_effects=True, vmem_limit_bytes=48 * 1024 * 1024
         ),
-    )(greens, mixing, occ, target, ordered, kernels, cos_table, sin_table)
+    )(
+        greens, broadening, occupation, neighbours, orbitals, blocks, phonon, mode_table,
+        cos_table, sin_table,
+    )
     return result.reshape(1, energies, atom_dev, 2, PAIR)
 
 

time: 125 us -> 125 us (level)
  other arithmetic: 6.24 us -> 0 us
  local copies, waits for them, and re-layouts: 6.26 us -> 9.29 us
  Pallas kernels: 112 us -> 115 us
    unnamed x3 -> x17, local copies, waits for them, and re-layouts: 1.4 us -> 7.71 us
    pallas_call x1, Pallas kernels: 112 us -> 115 us  [fused(): pl.pallas_call(functools.partial(fused_kernel, phases, shard_count, mom_c...]
    select_n x4 -> x0, other arithmetic: 2.86 us -> none  [the longest x1 2.15 us: fused(): ordered = jnp.where(keep, ordered, jnp.zeros((), coupling.dtype))]
    dynamic_slice x3 -> x0, local copies, waits for them, and re-layouts: 1.58 us -> none  [the longest x2 0.85 us: fused(): own_neighbours = lax.dynamic_slice_in_dim(neighbours, first_atom, atom_dev)]
where the time goes in v2:
time: 125 us; the launch traced here: 124 us
  Pallas kernels  115 us (92%)
  local copies, waits for them, and re-layouts  9.29 us (7%)
    pallas_call x1, Pallas kernels, fused(): pl.pallas_call(functools.partial(fused_kernel, phases, shard_count, mom_c...  115 us
    unnamed x17, local copies, waits for them, and re-layouts  7.71 us

profile of v2, /device:TPU:1, one launch (start us, length us, event | category | flops | bytes accessed | tf_op | source)
XLA Modules:
  0.0 124.4 jit_solution(5532717711596088702)
XLA Ops:
  0.0 0.8 copy.11.neighbours_ref
  0.8 0.0 copy-start
  0.8 1.6 %copy-done = bf16[4,4,256,256]{3,2,1,0:T(8,128)(2,1)S(1)} copy-done((bf16[4,4,256,256]{3,2,1,0:T(8,128)(2,1)S(1)}, bf16[4,4,256,256]{3,2,1,0:T(8,128)(2,1)}, u32[]{:S(2)}) %copy-start) | copy-done | bytes 2097176
  2.4 0.0 copy-start.1
  2.4 0.9 copy-done.1
  3.3 0.0 copy-start.2
  3.3 0.9 copy-done.2
  4.2 0.0 copy-start.3
  4.2 0.8 copy-done.3
  5.0 0.0 copy-start.4
  5.0 0.7 copy-done.4
  5.7 0.0 copy-start.5
  5.7 0.7 copy-done.5
  6.4 0.0 copy-start.6
  6.4 0.7 copy-done.6
  7.1 0.0 copy-start.7
  7.1 0.7 copy-done.7
  7.7 115.1 %shard_map.100 = bf16[256,2048]{1,0:T(8,128)(2,1)S(1)} custom-call(bf16[16,8,2,128,128]{4,3,2,1,0:T(8,128)(2,1)} %bitcast.3, bf16[2,128,128]{2,1,0:T(8,128)(2,1)S(1)} %copy-done.3, f32[1,16]{1,0:T(1,128)S(1)} %copy-done.6, s32[64,4]{1,0:T(8,128)S(1)} %copy.11.neighbours_ref, s32[64]{0:T(128)S(1)} %copy-done.7, bf16[4,4,16,16,256]{4,3,2,1,0:T(8,128)(2,1)S(1)} %bitcast.2, ...), custom_call_target="tpu_custom_call" | custom-call | tf_op jit(solution)/shard_map/pallas_call | solution.py:500
  122.8 1.6 %reshape.7 = bf16[1,256,4,2,256]{4,3,2,1,0:T(2,128)(2,1)} reshape(bf16[256,2048]{1,0:T(8,128)(2,1)S(1)} %shard_map.100) | data formatting | bytes 2097152 | tf_op jit(solution)/shard_map/reshape | solution.py:529
Async XLA Ops:
  0.8 1.6 %copy-start = (bf16[4,4,256,256]{3,2,1,0:T(8,128)(2,1)S(1)}, bf16[4,4,256,256]{3,2,1,0:T(8,128)(2,1)}, u32[]{:S(2)}) copy-start(bf16[4,4,256,256]{3,2,1,0:T(8,128)(2,1)} %param.15) | copy-start | bytes 6291460
  2.4 0.9 copy-start.1
  3.3 0.9 copy-start.2
  4.2 0.8 copy-start.3
  5.0 0.7 copy-start.4
  5.7 0.7 copy-start.5
  6.4 0.7 copy-start.6
  7.1 0.7 copy-start.7

commit v3 on v2

--- a/solution.py
+++ b/solution.py
@@ -129,9 +129,10 @@
 
 
 def phase_plan(atom_dev):
-    if atom_dev < 2:
-        return [(0, atom_dev)]
-    return [(0, atom_dev - 1), (atom_dev - 1, 1)]
+    if atom_dev < 4:
+        return [(start, 1) for start in range(atom_dev)]
+    first = atom_dev // 2
+    return [(0, first)] + [(start, 1) for start in range(first, atom_dev)]
 
 
 def fused_kernel(
@@ -139,16 +140,25 @@
     shard_count,
     mom_count,
     green_hbm,
+    broadening_hbm,
+    occupation_hbm,
+    neighbours_hbm,
+    orbitals_hbm,
+    coupling_hbm,
+    phonon_hbm,
+    modes_hbm,
+    cos_hbm,
+    sin_hbm,
+    out_ref,
     broadening_ref,
     occupation_ref,
     neighbours_ref,
     orbitals_ref,
-    coupling_hbm,
     phonon_ref,
     modes_ref,
     cos_ref,
     sin_ref,
-    out_ref,
+    small_sem,
     green_buf,
     full_buf,
     send_buf,
@@ -173,11 +183,12 @@
     half = layers // 2
     pieces = NORB // 2
     last = len(phases) - 1
+    early = min(2, len(phases))
 
     def layer_at(step):
         home = lax.div(me, dev_layer)
-        side = lax.rem(lax.div(home, half) + 1 + lax.div(step, half), 2)
-        return side * half + lax.rem(home + step, half)
+        side = lax.rem(lax.div(home, half) + 1 + step, 2)
+        return side * half + lax.rem(home + lax.div(step, 2), half)
 
     def green_copy(layer):
         return pltpu.make_async_copy(
@@ -233,8 +244,26 @@
             device_id_type=MESH,
         )
 
+    small = [
+        (broadening_hbm, broadening_ref),
+        (occupation_hbm, occupation_ref),
+        (neighbours_hbm, neighbours_ref),
+        (orbitals_hbm, orbitals_ref),
+        (phonon_hbm, phonon_ref),
+        (modes_hbm, modes_ref),
+        (cos_hbm, cos_ref),
+        (sin_hbm, sin_ref),
+    ]
+    small = [
+        pltpu.make_async_copy(source, held, small_sem.at[index])
+        for index, (source, held) in enumerate(small)
+    ]
+    for copy in small[:4]:
+        copy.start()
     for step in range(layers):
         green_copy(layer_at(step)).start()
+    for copy in small[4:]:
+        copy.start()
     for slot in range(NBR):
         coupling_copy(slot).start()
 
@@ -253,6 +282,8 @@
             device_id={"mom": lax.rem(mom + step, mom_count)},
             device_id_type=MESH,
         )
+    for copy in small[:4]:
+        copy.wait()
     mixing_ref[:ORB, :ORB] = broadening_ref[0]
     mixing_ref[:ORB, ORB:] = broadening_ref[1]
     mixing_ref[ORB:, :ORB] = -broadening_ref[1]
@@ -303,7 +334,7 @@
             atom = layer * ATL + slot
             target = lane_base
             for near in range(NBR):
-                start = (neighbours_ref[atom, near] - layer * ATL) * NORB
+                start = (neighbours_ref[near, atom] - layer * ATL) * NORB
                 target = target + jnp.where(lane_slot == near, start, 0)
             strips = []
             for part in range(2):
@@ -333,7 +364,8 @@
 
     def layer_step(step, carry):
         layer_pairs(layer_at(step))
-        start_sends(0, layer_at(step))
+        for phase in range(early):
+            start_sends(phase, layer_at(step))
         return carry
 
     def mask_coupling():
@@ -348,7 +380,7 @@
             own = orbitals_ref[place]
             kept = (outer < own) & (inner < own)
             masks = [
-                jnp.where(kept & (column < orbitals_ref[neighbours_ref[place, near]]), 1.0, 0.0)
+                jnp.where(kept & (column < orbitals_ref[neighbours_ref[near, place]]), 1.0, 0.0)
                 for near in range(NBR)
             ]
 
@@ -377,8 +409,8 @@
 
             @pl.when(dest != me)
             def _():
-                if phase > 0:
-                    send_copy(phase - 1, dest).wait_send()
+                if phase >= early:
+                    send_copy(phase - early, dest).wait_send()
                 send_copy(phase, dest).start()
 
             @pl.when(dest == me)
@@ -449,27 +481,40 @@
 
     layer_pairs(layer_at(0))
     pl.semaphore_wait(barrier, shard_count + mom_count - 2)
-    start_sends(0, layer_at(0))
+    for phase in range(early):
+        start_sends(phase, layer_at(0))
     lax.fori_loop(1, layers, layer_step, 0)
+    for copy in small[4:]:
+        copy.wait()
     mask_coupling()
     spread_phonon()
+
+    def send_phase(phase):
+        def more(step, carry):
+            start_sends(phase, layer_at(step))
+            return carry
+
+        lax.fori_loop(0, layers, more, 0)
+
+    done = 0
     for phase in range(len(phases)):
-        if phase < last:
-
-            def more(step, carry):
-                start_sends(phase + 1, layer_at(step))
-                return carry
-
-            lax.fori_loop(0, layers, more, 0)
+        if phase + 2 <= last and phase + 2 >= early:
+            send_phase(phase + 2)
         transform(phase)
-        if phase > 0:
-            finish(phase - 1)
+        if phase >= 2 or phase == last:
+            while done < phase:
+                finish(done)
+                done += 1
+        elif phase == 1:
+            finish(0)
+            done = 1
     finish(last)
 
     def drain(dest, carry):
         @pl.when(dest != me)
         def _():
-            send_copy(last, dest).wait_send()
+            for phase in range(max(len(phases) - early, 0), len(phases)):
+                send_copy(phase, dest).wait_send()
 
         return carry
 
@@ -495,14 +540,23 @@
     count = len(phases)
     vmem = pl.BlockSpec(memory_space=pltpu.VMEM)
     hbm = pl.BlockSpec(memory_space=pl.ANY)
-    smem = pl.BlockSpec(memory_space=pltpu.SMEM)
+    smem = pltpu.SMEM
     dma = pltpu.SemaphoreType.DMA
     result = pl.pallas_call(
         functools.partial(fused_kernel, phases, shard_count, mom_count),
         out_shape=jax.ShapeDtypeStruct((energies, atom_dev * 2 * PAIR), jnp.bfloat16),
-        in_specs=[hbm, vmem, smem, smem, smem, hbm, vmem, smem, vmem, vmem],
+        in_specs=[hbm] * 10,
         out_specs=vmem,
         scratch_shapes=[
+            pltpu.VMEM(broadening.shape, broadening.dtype),
+            smem(occupation.shape, occupation.dtype),
+            smem(neighbours.shape[::-1], neighbours.dtype),
+            smem(orbitals.shape, orbitals.dtype),
+            pltpu.VMEM(phonon.shape, phonon.dtype),
+            smem(mode_table.shape, mode_table.dtype),
+            pltpu.VMEM(cos_table.shape, cos_table.dtype),
+            pltpu.VMEM(sin_table.shape, sin_table.dtype),
+            dma((8,)),
             pltpu.VMEM((LAYERS, energy_dev, 2, ORB, ORB), jnp.bfloat16),
             pltpu.VMEM((2, energy_dev * ORB, ORB), jnp.float32),
             pltpu.VMEM((ATOMS, NORB, energy_dev, ORB), jnp.bfloat16),
@@ -520,10 +574,10 @@
             dma((count, max(mom_count - 1, 1))),
         ],
         compiler_params=pltpu.CompilerParams(
-            collective_id=0, has_side_effects=True, vmem_limit_bytes=48 * 1024 * 1024
+            collective_id=0, has_side_effects=True, vmem_limit_bytes=56 * 1024 * 1024
         ),
     )(
-        greens, broadening, occupation, neighbours, orbitals, blocks, phonon, mode_table,
+        greens, broadening, occupation, neighbours.T, orbitals, blocks, phonon, mode_table,
         cos_table, sin_table,
     )
     return result.reshape(1, energies, atom_dev, 2, PAIR)

time: 125 us -> 115 us (0.920)
  local copies, waits for them, and re-layouts: 9.29 us -> 2.61 us
  Pallas kernels: 115 us -> 112 us
    unnamed x17 -> x0, local copies, waits for them, and re-layouts: 7.71 us -> none
    pallas_call x1, Pallas kernels: 115 us -> 112 us  [fused(): pl.pallas_call(functools.partial(fused_kernel, phases, shard_count, mom_c...]
where the time goes in v3:
time: 115 us
  Pallas kernels  112 us (97%)
  local copies, waits for them, and re-layouts  2.61 us (2%)
    pallas_call x1, Pallas kernels, fused(): pl.pallas_call(functools.partial(fused_kernel, phases, shard_count, mom_c...  112 us
    reshape x1, local copies, waits for them, and re-layouts, fused(): return result.reshape(1, energies, atom_dev, 2, PAIR)  2.61 us

profile of v3, /device:TPU:1, one launch (start us, length us, event | category | flops | bytes accessed | tf_op | source)
XLA Modules:
  0.0 115.0 jit_solution(8509071595865830320)
XLA Ops:
  0.0 112.4 %shard_map.100 = bf16[256,2048]{1,0:T(8,128)(2,1)} custom-call(bf16[16,8,2,128,128]{4,3,2,1,0:T(8,128)(2,1)} %bitcast.3, bf16[2,128,128]{2,1,0:T(8,128)(2,1)} %broadening_hbm.1, f32[1,16]{1,0:T(1,128)} %occupation_hbm.1, s32[4,64]{1,0:T(4,128)} %bitcast.5, s32[64]{0:T(128)} %orbitals_hbm.1, bf16[4,4,16,16,256]{4,3,2,1,0:T(8,128)(2,1)} %bitcast.4, ...), custom_call_target="tpu_custom_call" | custom-call | tf_op jit(solution)/shard_map/pallas_call | solution.py:545
  112.4 2.6 %reshape.7 = bf16[1,256,4,2,256]{4,3,2,1,0:T(2,128)(2,1)} reshape(bf16[256,2048]{1,0:T(8,128)(2,1)} %shard_map.100) | data formatting | bytes 2097152 | tf_op jit(solution)/shard_map/reshape | solution.py:583

commit v4 on v3

--- a/solution.py
+++ b/solution.py
@@ -128,11 +128,8 @@
 MESH = pl.DeviceIdType.MESH
 
 
-def phase_plan(atom_dev):
-    if atom_dev < 4:
-        return [(start, 1) for start in range(atom_dev)]
-    first = atom_dev // 2
-    return [(0, first)] + [(start, 1) for start in range(first, atom_dev)]
+def phase_plan(atom_dev, shared):
+    return [(0, shared)] + [(start, 1) for start in range(shared, atom_dev)]
 
 
 def fused_kernel(
@@ -166,6 +163,9 @@
     coupling_buf,
     kernel_buf,
     mixing_ref,
+    mirror_buf,
+    coupled_buf,
+    part_buf,
     time_buf,
     green_sem,
     coupling_sem,
@@ -174,6 +174,10 @@
     recv_sem,
     mom_send_sem,
     mom_recv_sem,
+    mirror_sem,
+    forward_send_sem,
+    forward_recv_sem,
+    part_sem,
 ):
     me = lax.axis_index("shard")
     mom = lax.axis_index("mom")
@@ -184,6 +188,12 @@
     pieces = NORB // 2
     last = len(phases) - 1
     early = min(2, len(phases))
+    shared = phases[0][1]
+    half_count = shard_count // 2
+    my_half = lax.div(me, half_count)
+    my_rank = lax.rem(me, half_count)
+    mirror = lax.rem(me + half_count, shard_count)
+    half_rows = half_count * energy_dev
 
     def layer_at(step):
         home = lax.div(me, dev_layer)
@@ -195,37 +205,78 @@
             green_hbm.at[:, layer], green_buf.at[layer], green_sem.at[layer]
         )
 
-    def coupling_copy(slot):
+    def coupling_copy():
+        return pltpu.make_async_copy(coupling_hbm, coupling_buf, coupling_sem)
+
+    def mirror_copy():
+        return pltpu.make_async_remote_copy(
+            src_ref=coupling_hbm.at[mom],
+            dst_ref=mirror_buf.at[mom],
+            send_sem=mirror_sem.at[0],
+            recv_sem=mirror_sem.at[1],
+            device_id={"shard": mirror},
+            device_id_type=MESH,
+        )
+
+    def forward_copy(step, sending):
+        source = lax.rem(mom + mom_count - step, mom_count)
+        return pltpu.make_async_remote_copy(
+            src_ref=mirror_buf.at[mom],
+            dst_ref=mirror_buf.at[mom if sending else source],
+            send_sem=forward_send_sem.at[step - 1],
+            recv_sem=forward_recv_sem.at[step - 1],
+            device_id={"mom": lax.rem(mom + step, mom_count)},
+            device_id_type=MESH,
+        )
+
+    def part_copy(sending):
+        origin = my_half if sending else 1 - my_half
+        rows = pl.ds(pl.multiple_of(origin * half_rows, half_rows), half_rows)
+        return pltpu.make_async_remote_copy(
+            src_ref=part_buf,
+            dst_ref=coupled_buf.at[:, :, rows],
+            send_sem=part_sem.at[0],
+            recv_sem=part_sem.at[1],
+            device_id={"shard": mirror},
+            device_id_type=MESH,
+        )
+
+    def route(phase, dest):
+        if phase > 0:
+            return dest, me
+        crossing = lax.rem(my_half + lax.div(dest, half_count), 2)
+        target = my_half * half_count + lax.rem(dest, half_count)
+        return target, crossing * half_count + my_rank
+
+    def own_copy(phase, dest):
+        start, size = phases[phase]
+        slot = route(phase, dest)[1]
+        crossing = lax.rem(my_half + lax.div(dest, half_count), 2) if phase == 0 else 0
         return pltpu.make_async_copy(
-            coupling_hbm.at[:, slot], coupling_buf.at[:, :, slot], coupling_sem.at[slot]
-        )
-
-    def own_copy(phase):
-        start, size = phases[phase]
-        return pltpu.make_async_copy(
-            send_buf.at[pl.ds(me * atom_dev + start, size)],
-            recv_buf.at[pl.ds(start, size), me],
-            own_sem.at[phase],
+            send_buf.at[pl.ds(dest * atom_dev + start, size)],
+            recv_buf.at[pl.ds(start, size), slot],
+            own_sem.at[phase + crossing * len(phases)],
         )
 
     def send_copy(phase, dest):
         start, size = phases[phase]
+        target, slot = route(phase, dest)
         return pltpu.make_async_remote_copy(
             src_ref=send_buf.at[pl.ds(dest * atom_dev + start, size)],
-            dst_ref=recv_buf.at[pl.ds(start, size), me],
+            dst_ref=recv_buf.at[pl.ds(start, size), slot],
             send_sem=send_sem.at[phase, dest],
-            recv_sem=recv_sem.at[phase, me],
-            device_id={"shard": dest},
+            recv_sem=recv_sem.at[phase, slot],
+            device_id={"shard": target},
             device_id_type=MESH,
         )
 
-    def arrive_copy(phase, source):
+    def arrive_copy(phase, slot, source):
         start, size = phases[phase]
         return pltpu.make_async_remote_copy(
             src_ref=send_buf.at[pl.ds(source * atom_dev + start, size)],
-            dst_ref=recv_buf.at[pl.ds(start, size), source],
+            dst_ref=recv_buf.at[pl.ds(start, size), slot],
             send_sem=send_sem.at[phase, source],
-            recv_sem=recv_sem.at[phase, source],
+            recv_sem=recv_sem.at[phase, slot],
             device_id={"shard": source},
             device_id_type=MESH,
         )
@@ -264,8 +315,7 @@
         green_copy(layer_at(step)).start()
     for copy in small[4:]:
         copy.start()
-    for slot in range(NBR):
-        coupling_copy(slot).start()
+    coupling_copy().start()
 
     barrier = pltpu.get_barrier_semaphore()
     for step in range(1, shard_count):
@@ -288,6 +338,8 @@
     mixing_ref[:ORB, ORB:] = broadening_ref[1]
     mixing_ref[ORB:, :ORB] = -broadening_ref[1]
     mixing_ref[ORB:, ORB:] = broadening_ref[0]
+    pl.semaphore_wait(barrier, shard_count + mom_count - 2)
+    mirror_copy().start()
     group = 8
     unroll = 4
 
@@ -366,34 +418,35 @@
         layer_pairs(layer_at(step))
         for phase in range(early):
             start_sends(phase, layer_at(step))
+
+        @pl.when(step == layers - 2)
+        def _():
+            mirror_copy().wait_recv()
+            for other in range(1, mom_count):
+                forward_copy(other, True).start()
+
         return carry
 
-    def mask_coupling():
+    def mask_coupling(buffer, atom, place):
         shape = (NORB, PAIR)
         column = lax.broadcasted_iota(jnp.int32, shape, 0)
         entry = lax.broadcasted_iota(jnp.int32, shape, 1)
         outer, inner = lax.div(entry, NORB), lax.rem(entry, NORB)
-        for slot in range(NBR):
-            coupling_copy(slot).wait()
-        for atom in range(atom_dev):
-            place = me * atom_dev + atom
-            own = orbitals_ref[place]
-            kept = (outer < own) & (inner < own)
-            masks = [
-                jnp.where(kept & (column < orbitals_ref[neighbours_ref[near, place]]), 1.0, 0.0)
-                for near in range(NBR)
-            ]
-
-            def row_step(row, carry):
-                used = jnp.where(row < own, 1.0, 0.0)
-                for near in range(NBR):
-                    block = coupling_buf[atom, row, near].astype(jnp.float32)
-                    coupling_buf[atom, row, near] = (block * (masks[near] * used)).astype(
-                        jnp.bfloat16
-                    )
-                return carry
-
-            lax.fori_loop(0, NORB, row_step, 0)
+        own = orbitals_ref[place]
+        kept = (outer < own) & (inner < own)
+        masks = [
+            jnp.where(kept & (column < orbitals_ref[neighbours_ref[near, place]]), 1.0, 0.0)
+            for near in range(NBR)
+        ]
+
+        def row_step(row, carry):
+            used = jnp.where(row < own, 1.0, 0.0)
+            for near in range(NBR):
+                block = buffer[atom, near, row].astype(jnp.float32)
+                buffer[atom, near, row] = (block * (masks[near] * used)).astype(jnp.bfloat16)
+            return carry
+
+        lax.fori_loop(0, NORB, row_step, 0)
 
     def spread_phonon():
         for other in range(mom_count):
@@ -406,16 +459,22 @@
     def start_sends(phase, layer):
         for offset in range(dev_layer):
             dest = layer * dev_layer + offset
-
-            @pl.when(dest != me)
+            if phase >= early:
+                before = phase - early
+
+                @pl.when(route(before, dest)[0] != me)
+                def _():
+                    send_copy(before, dest).wait_send()
+
+            target = route(phase, dest)[0]
+
+            @pl.when(target != me)
             def _():
-                if phase >= early:
-                    send_copy(phase - early, dest).wait_send()
                 send_copy(phase, dest).start()
 
-            @pl.when(dest == me)
+            @pl.when(target == me)
             def _():
-                own_copy(phase).start()
+                own_copy(phase, dest).start()
 
     def finish(phase):
         start, size = phases[phase]
@@ -432,7 +491,6 @@
                 sums[1] = sums[1] + (wide_re * time_im + wide_im * time_re)
             conv_re = sums[0].astype(jnp.bfloat16)
             conv_im = sums[1].astype(jnp.bfloat16)
-            dot = functools.partial(jnp.dot, preferred_element_type=jnp.float32)
             scale = 1.0 / cos_ref.shape[0]
             res_re = (dot(cos_ref[...], conv_re) - dot(sin_ref[...], conv_im)) * scale
             res_im = (dot(cos_ref[...], conv_im) + dot(sin_ref[...], conv_re)) * scale
@@ -440,53 +498,95 @@
             out_ref[:, base : base + PAIR] = res_re.astype(jnp.bfloat16)
             out_ref[:, base + PAIR : base + 2 * PAIR] = res_im.astype(jnp.bfloat16)
 
+    dot = functools.partial(jnp.dot, preferred_element_type=jnp.float32)
+
+    def arrive_all(phase):
+        def arrive(slot, carry):
+            source = slot
+            if phase == 0:
+                source = my_half * half_count + lax.rem(slot, half_count)
+
+            @pl.when(source != me)
+            def _():
+                arrive_copy(phase, slot, source).wait_recv()
+
+            return carry
+
+        lax.fori_loop(0, shard_count, arrive, 0)
+        own_copy(phase, me).wait()
+        if phase == 0:
+            own_copy(phase, mirror).wait()
+
+    def couple(atom, weights, place, first, count):
+        result = []
+        for part in range(2):
+            total = 0.0
+            for piece in range(0, pieces, 2):
+                block = jnp.concatenate(
+                    [
+                        recv_buf[
+                            atom, first : first + count, part * pieces + piece + low
+                        ].reshape(count * energy_dev, ORB)
+                        for low in range(2)
+                    ],
+                    axis=1,
+                )
+                matrix = jnp.concatenate(
+                    [
+                        weights[place, near, row]
+                        for row in range(2 * piece, 2 * piece + 4)
+                        for near in range(NBR)
+                    ],
+                    axis=0,
+                )
+                total = total + dot(block, matrix)
+            result.append(total.astype(jnp.bfloat16))
+        return result
+
+    def to_time(atom, coupled):
+        time_re = dot(cos_ref[...], coupled[0]) + dot(sin_ref[...], coupled[1])
+        time_im = dot(cos_ref[...], coupled[1]) - dot(sin_ref[...], coupled[0])
+        time_buf[mom, atom, 0] = time_re.astype(jnp.bfloat16)
+        time_buf[mom, atom, 1] = time_im.astype(jnp.bfloat16)
+
+    def mirror_part():
+        for other in range(1, mom_count):
+            forward_copy(other, True).wait_send()
+            forward_copy(other, False).wait_recv()
+        for atom in range(shared):
+            mask_coupling(mirror_buf, atom, mirror * atom_dev + atom)
+        arrive_all(0)
+        for atom in range(shared):
+            far = couple(atom, mirror_buf, atom, half_count, half_count)
+            for part in range(2):
+                part_buf[atom, part] = far[part]
+        part_copy(True).start()
+        rows = pl.ds(pl.multiple_of(my_half * half_rows, half_rows), half_rows)
+        for atom in range(shared):
+            near = couple(atom, coupling_buf, atom, 0, half_count)
+            for part in range(2):
+                coupled_buf[atom, part, rows, :] = near[part]
+
     def transform(phase):
         start, size = phases[phase]
-
-        def arrive(source, carry):
-            @pl.when(source != me)
-            def _():
-                arrive_copy(phase, source).wait_recv()
-
-            return carry
-
-        lax.fori_loop(0, shard_count, arrive, 0)
-        own_copy(phase).wait()
-        energies = shard_count * energy_dev
-        for atom in range(start, start + size):
-            coupled = []
-            for part in range(2):
-                total = 0.0
-                for piece in range(0, pieces, 2):
-                    block = jnp.concatenate(
-                        [
-                            recv_buf[atom, :, part * pieces + piece + low].reshape(energies, ORB)
-                            for low in range(2)
-                        ],
-                        axis=1,
-                    )
-                    total = total + jnp.dot(
-                        block,
-                        coupling_buf[atom, 2 * piece : 2 * piece + 4].reshape(PAIR, PAIR),
-                        preferred_element_type=jnp.float32,
-                    )
-                coupled.append(total.astype(jnp.bfloat16))
-            dot = functools.partial(jnp.dot, preferred_element_type=jnp.float32)
-            time_re = dot(cos_ref[...], coupled[0]) + dot(sin_ref[...], coupled[1])
-            time_im = dot(cos_ref[...], coupled[1]) - dot(sin_ref[...], coupled[0])
-            time_buf[mom, atom, 0] = time_re.astype(jnp.bfloat16)
-            time_buf[mom, atom, 1] = time_im.astype(jnp.bfloat16)
+        if phase == 0:
+            mirror_part()
+            part_copy(False).wait_recv()
+            for atom in range(size):
+                to_time(atom, [coupled_buf[atom, 0], coupled_buf[atom, 1]])
+        else:
+            arrive_all(phase)
+            for atom in range(start, start + size):
+                to_time(atom, couple(atom, coupling_buf, atom, 0, shard_count))
         for step in range(1, mom_count):
             mom_copy(phase, step, True).start()
 
-    layer_pairs(layer_at(0))
-    pl.semaphore_wait(barrier, shard_count + mom_count - 2)
-    for phase in range(early):
-        start_sends(phase, layer_at(0))
-    lax.fori_loop(1, layers, layer_step, 0)
+    lax.fori_loop(0, layers, layer_step, 0)
     for copy in small[4:]:
         copy.wait()
-    mask_coupling()
+    coupling_copy().wait()
+    for atom in range(atom_dev):
+        mask_coupling(coupling_buf, atom, me * atom_dev + atom)
     spread_phonon()
 
     def send_phase(phase):
@@ -511,14 +611,17 @@
     finish(last)
 
     def drain(dest, carry):
-        @pl.when(dest != me)
-        def _():
-            for phase in range(max(len(phases) - early, 0), len(phases)):
+        for phase in range(max(len(phases) - early, 0), len(phases)):
+
+            @pl.when(route(phase, dest)[0] != me)
+            def _():
                 send_copy(phase, dest).wait_send()
 
         return carry
 
     lax.fori_loop(0, shard_count, drain, 0)
+    mirror_copy().wait_send()
+    part_copy(True).wait_send()
     for phase in range(len(phases)):
         for step in range(1, mom_count):
             mom_copy(phase, step, True).wait_send()
@@ -536,7 +639,8 @@
     cos_table = jnp.asarray(np.cos(angles), jnp.bfloat16)
     sin_table = jnp.asarray(np.sin(angles), jnp.bfloat16)
     blocks = coupling.reshape(atom_dev, NBR, NORB, NORB, PAIR)
-    phases = phase_plan(atom_dev)
+    shared = mom_count
+    phases = phase_plan(atom_dev, shared)
     count = len(phases)
     vmem = pl.BlockSpec(memory_space=pltpu.VMEM)
     hbm = pl.BlockSpec(memory_space=pl.ANY)
@@ -561,17 +665,24 @@
             pltpu.VMEM((2, energy_dev * ORB, ORB), jnp.float32),
             pltpu.VMEM((ATOMS, NORB, energy_dev, ORB), jnp.bfloat16),
             pltpu.VMEM((atom_dev, shard_count, NORB, energy_dev, ORB), jnp.bfloat16),
-            pltpu.VMEM((atom_dev, NORB, NBR, NORB, PAIR), jnp.bfloat16),
+            pltpu.VMEM((atom_dev, NBR, NORB, NORB, PAIR), jnp.bfloat16),
             pltpu.VMEM((mom_count, 2, energies, ORB), jnp.float32),
             pltpu.VMEM((2 * ORB, 2 * ORB), jnp.bfloat16),
+            pltpu.VMEM((shared, NBR, NORB, NORB, PAIR), jnp.bfloat16),
+            pltpu.VMEM((shared, 2, energies, PAIR), jnp.bfloat16),
+            pltpu.VMEM((shared, 2, energies // 2, PAIR), jnp.bfloat16),
             pltpu.VMEM((mom_count, atom_dev, 2, energies, PAIR), jnp.bfloat16),
             dma((LAYERS,)),
-            dma((NBR,)),
-            dma((count,)),
+            dma,
+            dma((2 * count,)),
             dma((count, shard_count)),
             dma((count, shard_count)),
             dma((count, max(mom_count - 1, 1))),
             dma((count, max(mom_count - 1, 1))),
+            dma((2,)),
+            dma((max(mom_count - 1, 1),)),
+            dma((max(mom_count - 1, 1),)),
+            dma((2,)),
         ],
         compiler_params=pltpu.CompilerParams(
             collective_id=0, has_side_effects=True, vmem_limit_bytes=56 * 1024 * 1024
@@ -599,7 +710,7 @@
 
     def body(*args):
         energy_dev, atom_dev = args[0].shape[1], args[5].shape[0]
-        if energy_dev % 16 == 0 and ATL % atom_dev == 0:
+        if energy_dev % 16 == 0 and ATL % atom_dev == 0 and atom_dev >= mom_count + 2:
             return fused(shard_count, mom_count, *args)
         return local(*args)
 

time: 115 us -> 119 us (1.035)
  Pallas kernels: 112 us -> 116 us
    pallas_call x1, Pallas kernels: 112 us -> 116 us  [fused(): pl.pallas_call(functools.partial(fused_kernel, phases, shard_count, mom_c...]
where the time goes in v4:
time: 119 us; the launch traced here: 118 us
  Pallas kernels  116 us (97%)
  local copies, waits for them, and re-layouts  2.61 us (2%)
    pallas_call x1, Pallas kernels, fused(): pl.pallas_call(functools.partial(fused_kernel, phases, shard_count, mom_c...  116 us
    reshape x1, local copies, waits for them, and re-layouts, fused(): return result.reshape(1, energies, atom_dev, 2, PAIR)  2.61 us

profile of v4, /device:TPU:1, one launch (start us, length us, event | category | flops | bytes accessed | tf_op | source)
XLA Modules:
  0.0 118.2 jit_solution(9335000420941710142)
XLA Ops:
  0.0 115.6 %shard_map.100 = bf16[256,2048]{1,0:T(8,128)(2,1)} custom-call(bf16[16,8,2,128,128]{4,3,2,1,0:T(8,128)(2,1)} %bitcast.3, bf16[2,128,128]{2,1,0:T(8,128)(2,1)} %broadening_hbm.1, f32[1,16]{1,0:T(1,128)} %occupation_hbm.1, s32[4,64]{1,0:T(4,128)} %bitcast.5, s32[64]{0:T(128)} %orbitals_hbm.1, bf16[4,4,16,16,256]{4,3,2,1,0:T(8,128)(2,1)} %bitcast.4, ...), custom_call_target="tpu_custom_call" | custom-call | tf_op jit(solution)/shard_map/pallas_call | solution.py:649
  115.6 2.6 %reshape.7 = bf16[1,256,4,2,256]{4,3,2,1,0:T(2,128)(2,1)} reshape(bf16[256,2048]{1,0:T(8,128)(2,1)} %shard_map.100) | data formatting | bytes 2097152 | tf_op jit(solution)/shard_map/reshape | solution.py:694

commit v5 on v4

--- a/solution.py
+++ b/solution.py
@@ -163,6 +163,7 @@
     coupling_buf,
     kernel_buf,
     mixing_ref,
+    turn_ref,
     mirror_buf,
     coupled_buf,
     part_buf,
@@ -340,6 +341,11 @@
     mixing_ref[ORB:, ORB:] = broadening_ref[0]
     pl.semaphore_wait(barrier, shard_count + mom_count - 2)
     mirror_copy().start()
+    turn_shape = turn_ref.shape
+    wanted = lax.broadcasted_iota(jnp.int32, turn_shape, 0)
+    held = lax.broadcasted_iota(jnp.int32, turn_shape, 1)
+    wanted = lax.rem(wanted, energy_dev) * NORB + lax.div(wanted, energy_dev)
+    turn_ref[...] = jnp.where(wanted == held, 1.0, 0.0).astype(jnp.bfloat16)
     group = 8
     unroll = 4
 
@@ -360,19 +366,18 @@
                 preferred_element_type=jnp.float32,
             ).astype(jnp.bfloat16)
             for j in range(group):
-                turned = jnp.concatenate(
-                    [-joined[j][:, ORB:], joined[j][:, :ORB]], axis=1
-                )
-                full = lax.dot_general(
-                    left[j * ORB : (j + 1) * ORB],
-                    jnp.concatenate([joined[j], turned], axis=0),
+                own_left = left[j * ORB : (j + 1) * ORB]
+                products = lax.dot_general(
+                    jnp.concatenate([own_left[:, :ORB], own_left[:, ORB:]], axis=0),
+                    jnp.concatenate([joined[j][:, :ORB], joined[j][:, ORB:]], axis=0),
                     (((1,), (1,)), ((), ())),
                     preferred_element_type=jnp.float32,
                 )
-                full = full * occupation_ref[0, first + j]
-                rows = pl.ds(pl.multiple_of((first + j) * ORB, ORB), ORB)
-                full_buf[0, rows, :] = full[:, :ORB]
-                full_buf[1, rows, :] = full[:, ORB:]
+                full_re = products[:ORB, :ORB] + products[ORB:, ORB:]
+                full_im = products[ORB:, :ORB] - products[:ORB, ORB:]
+                weight = occupation_ref[0, first + j]
+                full_buf[first + j, :, :ORB] = (full_re * weight).astype(jnp.bfloat16)
+                full_buf[first + j, :, ORB:] = (full_im * weight).astype(jnp.bfloat16)
             return inner
 
         lax.fori_loop(0, energy_dev // group, energy_step, 0)
@@ -388,15 +393,18 @@
             for near in range(NBR):
                 start = (neighbours_ref[near, atom] - layer * ATL) * NORB
                 target = target + jnp.where(lane_slot == near, start, 0)
+            rows = pl.ds(pl.multiple_of(slot * NORB, NORB), NORB)
+            block = full_buf[:, rows, :].reshape(energy_dev * NORB, 2 * ORB)
+            turned = jnp.dot(
+                turn_ref[...], block, preferred_element_type=jnp.float32
+            ).astype(jnp.bfloat16)
             strips = []
             for part in range(2):
+                columns = slice(part * ORB, (part + 1) * ORB)
                 for piece in range(pieces):
+                    begin = 2 * piece * energy_dev
                     pair = [
-                        full_buf[
-                            part,
-                            pl.ds(slot * NORB + 2 * piece + low, energy_dev, stride=ORB),
-                            :,
-                        ].astype(jnp.bfloat16)
+                        turned[begin + low * energy_dev : begin + (low + 1) * energy_dev, columns]
                         for low in range(2)
                     ]
                     strips.append(jnp.concatenate(pair, axis=1))
@@ -662,12 +670,13 @@
             pltpu.VMEM(sin_table.shape, sin_table.dtype),
             dma((8,)),
             pltpu.VMEM((LAYERS, energy_dev, 2, ORB, ORB), jnp.bfloat16),
-            pltpu.VMEM((2, energy_dev * ORB, ORB), jnp.float32),
+            pltpu.VMEM((energy_dev, ORB, 2 * ORB), jnp.bfloat16),
             pltpu.VMEM((ATOMS, NORB, energy_dev, ORB), jnp.bfloat16),
             pltpu.VMEM((atom_dev, shard_count, NORB, energy_dev, ORB), jnp.bfloat16),
             pltpu.VMEM((atom_dev, NBR, NORB, NORB, PAIR), jnp.bfloat16),
             pltpu.VMEM((mom_count, 2, energies, ORB), jnp.float32),
             pltpu.VMEM((2 * ORB, 2 * ORB), jnp.bfloat16),
+            pltpu.VMEM((energy_dev * NORB, energy_dev * NORB), jnp.bfloat16),
             pltpu.VMEM((shared, NBR, NORB, NORB, PAIR), jnp.bfloat16),
             pltpu.VMEM((shared, 2, energies, PAIR), jnp.bfloat16),
             pltpu.VMEM((shared, 2, energies // 2, PAIR), jnp.bfloat16),

time: 119 us -> 119 us (level)
  no operation moved by 1% of the time
where the time goes in v5:
time: 119 us; the launch traced here: 118 us
  Pallas kernels  116 us (97%)
  local copies, waits for them, and re-layouts  2.61 us (2%)
    pallas_call x1, Pallas kernels, fused(): pl.pallas_call(functools.partial(fused_kernel, phases, shard_count, mom_c...  116 us
    reshape x1, local copies, waits for them, and re-layouts, fused(): return result.reshape(1, energies, atom_dev, 2, PAIR)  2.61 us

profile of v5, /device:TPU:1, one launch (start us, length us, event | category | flops | bytes accessed | tf_op | source)
XLA Modules:
  0.0 118.2 jit_solution(7184750172745545199)
XLA Ops:
  0.0 115.6 %shard_map.100 = bf16[256,2048]{1,0:T(8,128)(2,1)} custom-call(bf16[16,8,2,128,128]{4,3,2,1,0:T(8,128)(2,1)} %bitcast.3, bf16[2,128,128]{2,1,0:T(8,128)(2,1)} %broadening_hbm.1, f32[1,16]{1,0:T(1,128)} %occupation_hbm.1, s32[4,64]{1,0:T(4,128)} %bitcast.5, s32[64]{0:T(128)} %orbitals_hbm.1, bf16[4,4,16,16,256]{4,3,2,1,0:T(8,128)(2,1)} %bitcast.4, ...), custom_call_target="tpu_custom_call" | custom-call | tf_op jit(solution)/shard_map/pallas_call | solution.py:657
  115.6 2.6 %reshape.7 = bf16[1,256,4,2,256]{4,3,2,1,0:T(2,128)(2,1)} reshape(bf16[256,2048]{1,0:T(8,128)(2,1)} %shard_map.100) | data formatting | bytes 2097152 | tf_op jit(solution)/shard_map/reshape | solution.py:703

commit v6 on v5

--- a/solution.py
+++ b/solution.py
@@ -569,6 +569,8 @@
             for part in range(2):
                 part_buf[atom, part] = far[part]
         part_copy(True).start()
+        for phase in range(early, len(phases)):
+            send_phase(phase, layers // 2, layers)
         rows = pl.ds(pl.multiple_of(my_half * half_rows, half_rows), half_rows)
         for atom in range(shared):
             near = couple(atom, coupling_buf, atom, 0, half_count)
@@ -578,7 +580,6 @@
     def transform(phase):
         start, size = phases[phase]
         if phase == 0:
-            mirror_part()
             part_copy(False).wait_recv()
             for atom in range(size):
                 to_time(atom, [coupled_buf[atom, 0], coupled_buf[atom, 1]])
@@ -589,6 +590,13 @@
         for step in range(1, mom_count):
             mom_copy(phase, step, True).start()
 
+    def send_phase(phase, first, stop):
+        def more(step, carry):
+            start_sends(phase, layer_at(step))
+            return carry
+
+        lax.fori_loop(first, stop, more, 0)
+
     lax.fori_loop(0, layers, layer_step, 0)
     for copy in small[4:]:
         copy.wait()
@@ -597,26 +605,16 @@
         mask_coupling(coupling_buf, atom, me * atom_dev + atom)
     spread_phonon()
 
-    def send_phase(phase):
-        def more(step, carry):
-            start_sends(phase, layer_at(step))
-            return carry
-
-        lax.fori_loop(0, layers, more, 0)
-
-    done = 0
-    for phase in range(len(phases)):
-        if phase + 2 <= last and phase + 2 >= early:
-            send_phase(phase + 2)
+    for phase in range(early, len(phases)):
+        send_phase(phase, 0, layers // 2)
+    mirror_part()
+    transform(1)
+    transform(0)
+    finish(1)
+    finish(0)
+    for phase in range(2, len(phases)):
         transform(phase)
-        if phase >= 2 or phase == last:
-            while done < phase:
-                finish(done)
-                done += 1
-        elif phase == 1:
-            finish(0)
-            done = 1
-    finish(last)
+        finish(phase)
 
     def drain(dest, carry):
         for phase in range(max(len(phases) - early, 0), len(phases)):

time: 119 us -> 122 us (1.025)
  the two profiles are of different devices: /device:TPU:1 before, /device:TPU:2 now
where the time goes in v6:
time: 122 us
  Pallas kernels  119 us (98%)
  local copies, waits for them, and re-layouts  2.61 us (2%)
    pallas_call x1, Pallas kernels, fused(): pl.pallas_call(functools.partial(fused_kernel, phases, shard_count, mom_c...  119 us
    reshape x1, local copies, waits for them, and re-layouts, fused(): return result.reshape(1, energies, atom_dev, 2, PAIR)  2.61 us

profile of v6, /device:TPU:2, one launch (start us, length us, event | category | flops | bytes accessed | tf_op | source)
XLA Modules:
  0.0 121.6 jit_solution(15818600552913024858)
XLA Ops:
  0.0 118.9 %shard_map.100 = bf16[256,2048]{1,0:T(8,128)(2,1)} custom-call(bf16[16,8,2,128,128]{4,3,2,1,0:T(8,128)(2,1)} %bitcast.3, bf16[2,128,128]{2,1,0:T(8,128)(2,1)} %broadening_hbm.1, f32[1,16]{1,0:T(1,128)} %occupation_hbm.1, s32[4,64]{1,0:T(4,128)} %bitcast.5, s32[64]{0:T(128)} %orbitals_hbm.1, bf16[4,4,16,16,256]{4,3,2,1,0:T(8,128)(2,1)} %bitcast.4, ...), custom_call_target="tpu_custom_call" | custom-call | tf_op jit(solution)/shard_map/pallas_call | solution.py:655
  118.9 2.6 %reshape.7 = bf16[1,256,4,2,256]{4,3,2,1,0:T(2,128)(2,1)} reshape(bf16[256,2048]{1,0:T(8,128)(2,1)} %shard_map.100) | data formatting | bytes 2097152 | tf_op jit(solution)/shard_map/reshape | solution.py:701

commit v7 on v3

--- a/solution.py
+++ b/solution.py
@@ -166,6 +166,7 @@
     coupling_buf,
     kernel_buf,
     mixing_ref,
+    turn_ref,
     time_buf,
     green_sem,
     coupling_sem,
@@ -288,6 +289,11 @@
     mixing_ref[:ORB, ORB:] = broadening_ref[1]
     mixing_ref[ORB:, :ORB] = -broadening_ref[1]
     mixing_ref[ORB:, ORB:] = broadening_ref[0]
+    turn_shape = turn_ref.shape
+    wanted = lax.broadcasted_iota(jnp.int32, turn_shape, 0)
+    held = lax.broadcasted_iota(jnp.int32, turn_shape, 1)
+    wanted = lax.rem(wanted, energy_dev) * NORB + lax.div(wanted, energy_dev)
+    turn_ref[...] = jnp.where(wanted == held, 1.0, 0.0).astype(jnp.bfloat16)
     group = 8
     unroll = 4
 
@@ -308,19 +314,18 @@
                 preferred_element_type=jnp.float32,
             ).astype(jnp.bfloat16)
             for j in range(group):
-                turned = jnp.concatenate(
-                    [-joined[j][:, ORB:], joined[j][:, :ORB]], axis=1
-                )
-                full = lax.dot_general(
-                    left[j * ORB : (j + 1) * ORB],
-                    jnp.concatenate([joined[j], turned], axis=0),
+                own_left = left[j * ORB : (j + 1) * ORB]
+                products = lax.dot_general(
+                    jnp.concatenate([own_left[:, :ORB], own_left[:, ORB:]], axis=0),
+                    jnp.concatenate([joined[j][:, :ORB], joined[j][:, ORB:]], axis=0),
                     (((1,), (1,)), ((), ())),
                     preferred_element_type=jnp.float32,
                 )
-                full = full * occupation_ref[0, first + j]
-                rows = pl.ds(pl.multiple_of((first + j) * ORB, ORB), ORB)
-                full_buf[0, rows, :] = full[:, :ORB]
-                full_buf[1, rows, :] = full[:, ORB:]
+                full_re = products[:ORB, :ORB] + products[ORB:, ORB:]
+                full_im = products[ORB:, :ORB] - products[:ORB, ORB:]
+                weight = occupation_ref[0, first + j]
+                full_buf[first + j, :, :ORB] = (full_re * weight).astype(jnp.bfloat16)
+                full_buf[first + j, :, ORB:] = (full_im * weight).astype(jnp.bfloat16)
             return inner
 
         lax.fori_loop(0, energy_dev // group, energy_step, 0)
@@ -336,15 +341,18 @@
             for near in range(NBR):
                 start = (neighbours_ref[near, atom] - layer * ATL) * NORB
                 target = target + jnp.where(lane_slot == near, start, 0)
+            rows = pl.ds(pl.multiple_of(slot * NORB, NORB), NORB)
+            block = full_buf[:, rows, :].reshape(energy_dev * NORB, 2 * ORB)
+            turned = jnp.dot(
+                turn_ref[...], block, preferred_element_type=jnp.float32
+            ).astype(jnp.bfloat16)
             strips = []
             for part in range(2):
+                columns = slice(part * ORB, (part + 1) * ORB)
                 for piece in range(pieces):
+                    begin = 2 * piece * energy_dev
                     pair = [
-                        full_buf[
-                            part,
-                            pl.ds(slot * NORB + 2 * piece + low, energy_dev, stride=ORB),
-                            :,
-                        ].astype(jnp.bfloat16)
+                        turned[begin + low * energy_dev : begin + (low + 1) * energy_dev, columns]
                         for low in range(2)
                     ]
                     strips.append(jnp.concatenate(pair, axis=1))
@@ -558,12 +566,13 @@
             pltpu.VMEM(sin_table.shape, sin_table.dtype),
             dma((8,)),
             pltpu.VMEM((LAYERS, energy_dev, 2, ORB, ORB), jnp.bfloat16),
-            pltpu.VMEM((2, energy_dev * ORB, ORB), jnp.float32),
+            pltpu.VMEM((energy_dev, ORB, 2 * ORB), jnp.bfloat16),
             pltpu.VMEM((ATOMS, NORB, energy_dev, ORB), jnp.bfloat16),
             pltpu.VMEM((atom_dev, shard_count, NORB, energy_dev, ORB), jnp.bfloat16),
             pltpu.VMEM((atom_dev, NORB, NBR, NORB, PAIR), jnp.bfloat16),
             pltpu.VMEM((mom_count, 2, energies, ORB), jnp.float32),
             pltpu.VMEM((2 * ORB, 2 * ORB), jnp.bfloat16),
+            pltpu.VMEM((energy_dev * NORB, energy_dev * NORB), jnp.bfloat16),
             pltpu.VMEM((mom_count, atom_dev, 2, energies, PAIR), jnp.bfloat16),
             dma((LAYERS,)),
             dma((NBR,)),

time: 115 us -> 115 us (level)
  no operation moved by 1% of the time
where the time goes in v7:
time: 115 us
  Pallas kernels  112 us (97%)
  local copies, waits for them, and re-layouts  2.61 us (2%)
    pallas_call x1, Pallas kernels, fused(): pl.pallas_call(functools.partial(fused_kernel, phases, shard_count, mom_c...  112 us
    reshape x1, local copies, waits for them, and re-layouts, fused(): return result.reshape(1, energies, atom_dev, 2, PAIR)  2.61 us

profile of v7, /device:TPU:1, one launch (start us, length us, event | category | flops | bytes accessed | tf_op | source)
XLA Modules:
  0.0 115.1 jit_solution(10639426009603646468)
XLA Ops:
  0.0 112.5 %shard_map.100 = bf16[256,2048]{1,0:T(8,128)(2,1)} custom-call(bf16[16,8,2,128,128]{4,3,2,1,0:T(8,128)(2,1)} %bitcast.3, bf16[2,128,128]{2,1,0:T(8,128)(2,1)} %broadening_hbm.1, f32[1,16]{1,0:T(1,128)} %occupation_hbm.1, s32[4,64]{1,0:T(4,128)} %bitcast.5, s32[64]{0:T(128)} %orbitals_hbm.1, bf16[4,4,16,16,256]{4,3,2,1,0:T(8,128)(2,1)} %bitcast.4, ...), custom_call_target="tpu_custom_call" | custom-call | tf_op jit(solution)/shard_map/pallas_call | solution.py:553
  112.5 2.6 %reshape.7 = bf16[1,256,4,2,256]{4,3,2,1,0:T(2,128)(2,1)} reshape(bf16[256,2048]{1,0:T(8,128)(2,1)} %shard_map.100) | data formatting | bytes 2097152 | tf_op jit(solution)/shard_map/reshape | solution.py:592
